TPU v7x, 32 devices: a whole 2x2x4 slice. The times are simulated.
32 devices in a mesh: lat: 4 (over z), lon: 8 (over y, x, core).
Axes of the slice: x: 2, y: 2, z: 4, core: 2. Of those that a mesh axis runs over, the one named last changes fastest.
Arguments:
- corona: float32 [8, 64, 128, 128], P(None, 'lat', 'lon'), may hold values from -6 to 6
- kappa: float32 [64, 128, 128], P('lat', 'lon'), may hold values from 0.05 to 1
- mixing: float32 [8, 8], replicated, may hold values from -2 to 2
- helio_prev: float32 [8, 256, 512], P(None, 'lon', 'lat'), may hold values from -6 to 6
- owner: int32 [65536, 1], P(('lat', 'lon')), may hold values from 0 to 31; in each aligned block of 2048 rows (0 to 2047, 2048 to 4095, ...) at most 128 rows name the same one
- dest_cell: int32 [65536], P(('lat', 'lon')), may hold values from 0 to 4095
- corner_base: int32 [65536], P(('lat', 'lon')), may hold values from 0 to 1910, as said below
- fractions: float32 [3, 65536], P(None, ('lat', 'lon')), may hold values from 0 to 1
Outputs:
- stepped: float32 [8, 64, 128, 128], P(None, 'lat', 'lon')
- helio_face: float32 [8, 256, 512], P(None, 'lon', 'lat')
Inputs may be any that keep to these rules, and one draw needn't show every extreme that they name: Among the targets of one device no owner appears more than 128 times, a bound that some block reaches. corner_base = (t * 16 + p) * 8 + r with t < 15, p < 15, r < 7.
All inputs are finite; a program needn't handle non-finite values.
Results may differ from a plain program's by a relative error of at most 0.000075.
Values sent between devices are 32-bit elements; how exact they have to be, the bound alone decides.
A program may use at most 64 MiB of HBM per device.

v0:
```python
import jax
import jax.numpy as jnp
from jax import lax
from jax.sharding import PartitionSpec as P

SH = 8


def extended(block, sides, width):
    for axis, dim in sides:
        count = lax.axis_size(axis)
        forward = [(i, i + 1) for i in range(count - 1)]
        backward = [(target, source) for source, target in forward]
        low = lax.ppermute(
            lax.slice_in_dim(block, block.shape[dim] - width, None, axis=dim), axis, forward
        )
        high = lax.ppermute(lax.slice_in_dim(block, 0, width, axis=dim), axis, backward)
        block = jnp.concatenate([low, block, high], axis=dim)
    return block


def shift_last(array, step):
    zero_col = jnp.zeros(array.shape[:-1] + (1,), array.dtype)
    if step > 0:
        return jnp.concatenate([array[..., 1:], zero_col], axis=-1)
    return jnp.concatenate([zero_col, array[..., :-1]], axis=-1)


def flux_step(field, cond, mixing):
    center = field[:, 1:-1, 1:-1, :]
    cond_c = cond[1:-1, 1:-1, :]
    pairs = [
        (field[:, 2:, 1:-1, :], cond[2:, 1:-1, :]),
        (field[:, :-2, 1:-1, :], cond[:-2, 1:-1, :]),
        (field[:, 1:-1, 2:, :], cond[1:-1, 2:, :]),
        (field[:, 1:-1, :-2, :], cond[1:-1, :-2, :]),
        (shift_last(center, 1), shift_last(cond_c, 1)),
        (shift_last(center, -1), shift_last(cond_c, -1)),
    ]
    lapl = jnp.zeros_like(center)
    for near, cond_n in pairs:
        lapl = lapl + (0.5 * (cond_c + cond_n))[None] * (near - center)
    mixed = jnp.einsum("gf,fabr->gabr", mixing, center, precision=lax.Precision.HIGHEST)
    return center + 0.15 * lapl + 0.3 * mixed


def body(corona, kappa, mixing, helio_prev, owner, dest_cell, corner_base, fractions):
    fields, tile_t, tile_p, radial_n = corona.shape
    stacked = jnp.concatenate([corona, kappa[None]], axis=0)
    wide = extended(stacked, (("lat", 1), ("lon", 2)), 1)
    cond_wide = wide[fields]
    first = flux_step(wide[:fields], cond_wide, mixing)
    again = extended(first, (("lat", 1), ("lon", 2)), 1)
    stepped = flux_step(again, cond_wide, mixing)
    shell_cells = tile_t * tile_p * SH
    shell = stepped[:, :, :, radial_n - SH :].reshape(fields, shell_cells)
    count = corner_base.shape[0]
    blocksz = min(512, count)
    nblocks = count // blocksz
    cell_iota = jnp.arange(shell_cells, dtype=jnp.int32)
    base_blocks = corner_base.reshape(nblocks, blocksz)
    frac_blocks = jnp.transpose(fractions.reshape(3, nblocks, blocksz), (1, 0, 2))

    def interpolate(pair):
        base, frac = pair
        table = jnp.zeros((blocksz, shell_cells), jnp.float32)
        for a in range(2):
            for b in range(2):
                for c in range(2):
                    weight = (
                        (frac[0] if a else 1.0 - frac[0])
                        * (frac[1] if b else 1.0 - frac[1])
                        * (frac[2] if c else 1.0 - frac[2])
                    )
                    offset = (a * tile_p + b) * SH + c
                    table = table + jnp.where(
                        cell_iota[None, :] == (base + offset)[:, None], weight[:, None], 0.0
                    )
        return lax.dot_general(
            shell,
            table,
            (((1,), (1,)), ((), ())),
            precision=lax.Precision.HIGHEST,
            preferred_element_type=jnp.float32,
        )

    value_blocks = lax.map(interpolate, (base_blocks, frac_blocks))
    n_lat = lax.axis_size("lat")
    n_lon = lax.axis_size("lon")
    n_dev = n_lat * n_lon
    slots_each = 2 * count // n_dev
    n_slots = n_dev * slots_each
    dest_owner = owner[:, 0]
    hits = (dest_owner[:, None] == jnp.arange(n_dev, dtype=jnp.int32)[None, :]).astype(jnp.int32)
    rank = jnp.sum(jnp.cumsum(hits, axis=0) * hits, axis=1) - 1
    slot_blocks = (dest_owner * slots_each + rank).reshape(nblocks, blocksz)
    dest_blocks = (dest_cell + 1).astype(jnp.float32).reshape(nblocks, 1, blocksz)
    slot_iota = jnp.arange(n_slots, dtype=jnp.int32)

    def pack(total, items):
        vals, dests, slots = items
        placing = (slots[:, None] == slot_iota[None, :]).astype(jnp.float32)
        rows = jnp.concatenate([vals, dests], axis=0)
        return (
            total
            + jnp.dot(
                rows, placing, precision=lax.Precision.HIGHEST, preferred_element_type=jnp.float32
            ),
            None,
        )

    packed, _ = lax.scan(
        pack,
        jnp.zeros((fields + 1, n_slots), jnp.float32),
        (value_blocks, dest_blocks, slot_blocks),
    )
    face_p, face_t = (helio_prev.shape[1], helio_prev.shape[2])
    cells = face_p * face_t
    send_vals = packed[:fields]
    dest_plus = packed[fields].astype(jnp.int32)
    send_dest = jnp.where(dest_plus > 0, dest_plus - 1, cells)
    got_vals, got_dest = (
        lax.all_to_all(
            lax.all_to_all(
                send_vals.reshape(fields, n_lat, n_lon * slots_each),
                "lat",
                split_axis=1,
                concat_axis=1,
                tiled=True,
            ),
            "lon",
            split_axis=2,
            concat_axis=2,
            tiled=True,
        ),
        lax.all_to_all(
            lax.all_to_all(
                send_dest.reshape(1, n_lat, n_lon * slots_each),
                "lat",
                split_axis=1,
                concat_axis=1,
                tiled=True,
            ),
            "lon",
            split_axis=2,
            concat_axis=2,
            tiled=True,
        ),
    )
    recv_block = min(512, n_slots)
    recv_n = n_slots // recv_block
    recv_vals = jnp.transpose(got_vals.reshape(fields, recv_n, recv_block), (1, 0, 2))
    recv_dest = got_dest.reshape(recv_n, recv_block)
    face_iota = jnp.arange(cells, dtype=jnp.int32)

    def land(total, items):
        vals, dests = items
        placing = (dests[:, None] == face_iota[None, :]).astype(jnp.float32)
        return (
            total
            + jnp.dot(
                vals, placing, precision=lax.Precision.HIGHEST, preferred_element_type=jnp.float32
            ),
            None,
        )

    added, _ = lax.scan(land, jnp.zeros((fields, cells), jnp.float32), (recv_vals, recv_dest))
    coupled = helio_prev + added.reshape(fields, face_p, face_t)
    ext = extended(coupled, (("lat", 2), ("lon", 1)), 1)
    helio_face = coupled + 0.2 * (
        ext[:, 2:, 1:-1] + ext[:, :-2, 1:-1] + ext[:, 1:-1, 2:] + ext[:, 1:-1, :-2] - 4.0 * coupled
    )
    return (stepped, helio_face)


def solution(mesh):
    return jax.shard_map(
        body,
        mesh=mesh,
        in_specs=(
            P(None, "lat", "lon", None),
            P("lat", "lon", None),
            P(),
            P(None, "lon", "lat"),
            P(("lat", "lon"), None),
            P(("lat", "lon")),
            P(("lat", "lon")),
            P(None, ("lat", "lon")),
        ),
        out_specs=(P(None, "lat", "lon", None), P(None, "lon", "lat")),
        check_vma=False,
    )
```

profile of v0, /device:TPU:0, one launch (start us, length us, event | category | flops | bytes accessed | tf_op | source)
XLA Modules:
  0.0 189.0 jit_solution(9156598385317071077)
XLA Ops:
  3.3 4.9 %collective-permute-start = (f32[9,1,16,128]{3,0,2,1:T(8,128)S(1)}, f32[9,1,16,128]{3,0,2,1:T(8,128)S(1)}, u32[]{:S(2)}, u32[]{:S(2)}) collective-permute-start(f32[9,1,16,128]{3,0,2,1:T(8,128)S(1)} %get-tuple-element.256), channel_id=1, source_target_pairs={{0,8},{8,16},{16,24},{1,9},{9,17},{17,25},{2,10},{10,18},{18,26},{... | collective-permute-start | bytes 221192 | tf_op jit(solution)/shard_map/ppermute | solution.py:14
  10.9 9.1 %reduce-window.6 = s32[32,16,128]{2,1,0:T(8,128)S(1)} reduce-window(s32[32,16,128]{2,1,0:T(8,128)S(1)} %fusion.94, s32[]{:T(128)} %constant.52.clone.1), window={size=1x1x128 pad=0_0x0_0x127_0}, to_apply=%region_2.3 | reduce-window | flops 8323072 | bytes 524292 | tf_op jit(solution)/shard_map/reduce-window
  27.9 3.1 %fusion.61 = f32[8,16,16,128]{3,0,2,1:T(8,128)S(1)} fusion(f32[8,16,16,128]{3,0,2,1:T(8,128)S(1)} %copy.82, f32[9,18,1,128]{3,0,2,1:T(8,128)} %copy-done.3, f32[9,1,16,128]{3,0,2,1:T(8,128)S(1)} %collective-permute-done.1, f32[9,1,16,128]{3,0,2,1:T(8,128)S(1)} %collective-permute-done, f32[1,16,16,128]{3,0,2,1:T(1,128)S(1)} %bitcast.107, ...), kind=kOutput, calls=%fused_computation.91 | convolution fusion | flops 33816576 | bytes 5409024 | tf_op jit(solution)/shard_map/gf,fabr->gabr/dot_general | solution.py:43
  32.6 5.2 %collective-permute-start.5 = (f32[8,1,16,128]{3,0,2,1:T(8,128)S(1)}, f32[8,1,16,128]{3,0,2,1:T(8,128)S(1)}, u32[]{:S(2)}, u32[]{:S(2)}) collective-permute-start(f32[8,1,16,128]{3,0,2,1:T(8,128)S(1)} %get-tuple-element.260), channel_id=1, source_target_pairs={{0,8},{8,16},{16,24},{1,9},{9,17},{17,25},{2,10},{10,18},{18,26},{... | collective-permute-start | bytes 196616 | tf_op jit(solution)/shard_map/ppermute | solution.py:14
  40.9 5.4 %collective-permute-start.7 = (f32[8,18,1,128]{3,0,2,1:T(8,128)S(1)}, f32[8,18,1,128]{3,0,2,1:T(8,128)S(1)}, u32[]{:S(2)}, u32[]{:S(2)}) collective-permute-start(f32[8,18,1,128]{3,0,2,1:T(8,128)S(1)} %get-tuple-element.255), channel_id=1, source_target_pairs={{0,1},{1,2},{2,3},{3,4},{4,5},{5,6},{6,7},{8,9},{9,10},{10,11},{11... | collective-permute-start | bytes 221192 | tf_op jit(solution)/shard_map/ppermute | solution.py:14
  50.1 37.7 %while.34 = (s32[]{:T(128)}, f32[4,8,512]{2,1,0:T(8,128)S(1)}, s32[4,512]{1,0:T(4,128)}, f32[4,3,512]{2,1,0:T(4,128)}, f32[8,2048]{1,0:T(8,128)S(1)}, /*index=5*/s32[]{:T(128)}, s32[]{:T(128)}, s32[]{}, s32[]{}) while((s32[]{:T(128)}, f32[4,8,512]{2,1,0:T(8,128)S(1)}, s32[4,512]{1,0:T(4,128)}, f32[4,3,512]{2,1,0:T(4,128)}, ...), condition=%wide.region_1.2_spmd.clone.clone, body=%wide.region_0.1_spmd.clone.clone.sunk | while | flops 124791808 | bytes 8558729 | solution.py:87
  51.9 4.2 %fusion.129 = f32[512,2048]{1,0:T(8,128)S(1)} fusion(f32[512]{0:T(512)S(1)} %get-tuple-element.375, s32[512]{0:T(512)S(1)} %get-tuple-element.376, f32[512]{0:T(512)S(1)} %get-tuple-element.377, s32[512]{0:T(512)S(1)} %get-tuple-element.378, f32[512]{0:T(512)S(1)} %get-tuple-element.379, ...), kind=kLoop, calls=%fused_computation.12.clone.clone.clone.clone.clone.1.clone.1 | loop fusion | flops 24117248 | bytes 4227072 | tf_op jit(solution)/shard_map/while/body/eval_jaxpr/dot_general | solution.py:79
  56.1 3.6 %fusion.130 = f32[4,8,512]{2,1,0:T(8,128)S(1)} fusion(f32[4,8,512]{2,1,0:T(8,128)S(1)} %get-tuple-element.409, s32[]{:T(128)} %get-tuple-element.408, f32[8,2048]{1,0:T(8,128)S(1)} %get-tuple-element.421, f32[512,2048]{1,0:T(8,128)S(1)} %fusion.129), kind=kOutput, calls=%fused_computation.45.clone.2 | convolution fusion | flops 100663296 | bytes 4276228 | tf_op jit(solution)/shard_map/while/body/eval_jaxpr/dot_general | solution.py:79
  61.3 4.2 %fusion.129 = f32[512,2048]{1,0:T(8,128)S(1)} fusion(f32[512]{0:T(512)S(1)} %get-tuple-element.375, s32[512]{0:T(512)S(1)} %get-tuple-element.376, f32[512]{0:T(512)S(1)} %get-tuple-element.377, s32[512]{0:T(512)S(1)} %get-tuple-element.378, f32[512]{0:T(512)S(1)} %get-tuple-element.379, ...), kind=kLoop, calls=%fused_computation.12.clone.clone.clone.clone.clone.1.clone.1 | loop fusion | flops 24117248 | bytes 4227072 | tf_op jit(solution)/shard_map/while/body/eval_jaxpr/dot_general | solution.py:79
  65.4 3.6 %fusion.130 = f32[4,8,512]{2,1,0:T(8,128)S(1)} fusion(f32[4,8,512]{2,1,0:T(8,128)S(1)} %get-tuple-element.409, s32[]{:T(128)} %get-tuple-element.408, f32[8,2048]{1,0:T(8,128)S(1)} %get-tuple-element.421, f32[512,2048]{1,0:T(8,128)S(1)} %fusion.129), kind=kOutput, calls=%fused_computation.45.clone.2 | convolution fusion | flops 100663296 | bytes 4276228 | tf_op jit(solution)/shard_map/while/body/eval_jaxpr/dot_general | solution.py:79
  70.6 4.2 %fusion.129 = f32[512,2048]{1,0:T(8,128)S(1)} fusion(f32[512]{0:T(512)S(1)} %get-tuple-element.375, s32[512]{0:T(512)S(1)} %get-tuple-element.376, f32[512]{0:T(512)S(1)} %get-tuple-element.377, s32[512]{0:T(512)S(1)} %get-tuple-element.378, f32[512]{0:T(512)S(1)} %get-tuple-element.379, ...), kind=kLoop, calls=%fused_computation.12.clone.clone.clone.clone.clone.1.clone.1 | loop fusion | flops 24117248 | bytes 4227072 | tf_op jit(solution)/shard_map/while/body/eval_jaxpr/dot_general | solution.py:79
  74.8 3.6 %fusion.130 = f32[4,8,512]{2,1,0:T(8,128)S(1)} fusion(f32[4,8,512]{2,1,0:T(8,128)S(1)} %get-tuple-element.409, s32[]{:T(128)} %get-tuple-element.408, f32[8,2048]{1,0:T(8,128)S(1)} %get-tuple-element.421, f32[512,2048]{1,0:T(8,128)S(1)} %fusion.129), kind=kOutput, calls=%fused_computation.45.clone.2 | convolution fusion | flops 100663296 | bytes 4276228 | tf_op jit(solution)/shard_map/while/body/eval_jaxpr/dot_general | solution.py:79
  80.0 4.2 %fusion.129 = f32[512,2048]{1,0:T(8,128)S(1)} fusion(f32[512]{0:T(512)S(1)} %get-tuple-element.375, s32[512]{0:T(512)S(1)} %get-tuple-element.376, f32[512]{0:T(512)S(1)} %get-tuple-element.377, s32[512]{0:T(512)S(1)} %get-tuple-element.378, f32[512]{0:T(512)S(1)} %get-tuple-element.379, ...), kind=kLoop, calls=%fused_computation.12.clone.clone.clone.clone.clone.1.clone.1 | loop fusion | flops 24117248 | bytes 4227072 | tf_op jit(solution)/shard_map/while/body/eval_jaxpr/dot_general | solution.py:79
  84.2 3.6 %fusion.130 = f32[4,8,512]{2,1,0:T(8,128)S(1)} fusion(f32[4,8,512]{2,1,0:T(8,128)S(1)} %get-tuple-element.409, s32[]{:T(128)} %get-tuple-element.408, f32[8,2048]{1,0:T(8,128)S(1)} %get-tuple-element.421, f32[512,2048]{1,0:T(8,128)S(1)} %fusion.129), kind=kOutput, calls=%fused_computation.45.clone.2 | convolution fusion | flops 100663296 | bytes 4276228 | tf_op jit(solution)/shard_map/while/body/eval_jaxpr/dot_general | solution.py:79
  87.8 13.9 %while.35 = (s32[]{:T(128)}, f32[9,4096]{1,0:T(8,128)S(1)}, f32[4,8,512]{2,1,0:T(8,128)S(1)}, f32[4,1,512]{2,1,0:T(1,128)}, s32[4,512]{1,0:T(4,128)S(1)}, /*index=5*/s32[]{:T(128)}, s32[]{:T(128)}) while((s32[]{:T(128)}, f32[9,4096]{1,0:T(8,128)S(1)}, f32[4,8,512]{2,1,0:T(8,128)S(1)}, f32[4,1,512]{2,1,0:T(1,128)}, ...), condition=%wide.region_6.7_spmd.clone, body=%wide.region_5.6_spmd.clone.sunk | while | flops 228667904 | bytes 356451 | solution.py:112
  88.6 2.8 %fusion.132 = f32[9,4096]{1,0:T(8,128)S(1)} fusion(s32[512]{0:T(512)S(1)} %bitcast.120, f32[9,4096]{1,0:T(8,128)S(1)} %get-tuple-element.434, pred[]{:T(512)S(6)} %compare.12, f32[1,512]{1,0:T(1,128)S(1)} %dynamic-slice_bitcast_fusion.4, f32[8,512]{1,0:T(8,128)S(1)} %dynamic-slice_bitcast_fusion.5), kind=kOutput, calls=%fused_computation.71.clone.1 | convolution fusion | flops 228667904 | bytes 315393 | tf_op jit(solution)/shard_map/while/body/eval_jaxpr/dot_general | solution.py:106
  92.0 2.8 %fusion.132 = f32[9,4096]{1,0:T(8,128)S(1)} fusion(s32[512]{0:T(512)S(1)} %bitcast.120, f32[9,4096]{1,0:T(8,128)S(1)} %get-tuple-element.434, pred[]{:T(512)S(6)} %compare.12, f32[1,512]{1,0:T(1,128)S(1)} %dynamic-slice_bitcast_fusion.4, f32[8,512]{1,0:T(8,128)S(1)} %dynamic-slice_bitcast_fusion.5), kind=kOutput, calls=%fused_computation.71.clone.1 | convolution fusion | flops 228667904 | bytes 315393 | tf_op jit(solution)/shard_map/while/body/eval_jaxpr/dot_general | solution.py:106
  95.5 2.8 %fusion.132 = f32[9,4096]{1,0:T(8,128)S(1)} fusion(s32[512]{0:T(512)S(1)} %bitcast.120, f32[9,4096]{1,0:T(8,128)S(1)} %get-tuple-element.434, pred[]{:T(512)S(6)} %compare.12, f32[1,512]{1,0:T(1,128)S(1)} %dynamic-slice_bitcast_fusion.4, f32[8,512]{1,0:T(8,128)S(1)} %dynamic-slice_bitcast_fusion.5), kind=kOutput, calls=%fused_computation.71.clone.1 | convolution fusion | flops 228667904 | bytes 315393 | tf_op jit(solution)/shard_map/while/body/eval_jaxpr/dot_general | solution.py:106
  99.0 2.8 %fusion.132 = f32[9,4096]{1,0:T(8,128)S(1)} fusion(s32[512]{0:T(512)S(1)} %bitcast.120, f32[9,4096]{1,0:T(8,128)S(1)} %get-tuple-element.434, pred[]{:T(512)S(6)} %compare.12, f32[1,512]{1,0:T(1,128)S(1)} %dynamic-slice_bitcast_fusion.4, f32[8,512]{1,0:T(8,128)S(1)} %dynamic-slice_bitcast_fusion.5), kind=kOutput, calls=%fused_computation.71.clone.1 | convolution fusion | flops 228667904 | bytes 315393 | tf_op jit(solution)/shard_map/while/body/eval_jaxpr/dot_general | solution.py:106
  102.4 5.5 %all-to-all-start.2 = ((s32[1,4,1024]{2,0,1:T(1,128)}), s32[1,4,1024]{2,0,1:T(1,128)S(1)}, u32[]{:S(2)}, u32[]{:S(2)}) async-start(s32[1,4,1024]{2,0,1:T(1,128)} %bitcast.15), calls=%async_computation.2 | async-start | bytes 32768 | tf_op jit(solution)/shard_map/all_to_all | solution.py:137
  108.6 4.9 %all-to-all-done.2 = s32[1,4,1024]{2,0,1:T(1,128)S(1)} async-done(((s32[1,4,1024]{2,0,1:T(1,128)}), s32[1,4,1024]{2,0,1:T(1,128)S(1)}, u32[]{:S(2)}, u32[]{:S(2)}) %all-to-all-start.2) | async-done | bytes 16416 | tf_op jit(solution)/shard_map/all_to_all | solution.py:137
  113.5 3.5 %all-to-all-start = ((f32[8,4,1024]{2,0,1:T(8,128)}), f32[8,4,1024]{2,0,1:T(8,128)S(1)}, u32[]{:S(2)}, u32[]{:S(2)}) async-start(f32[8,4,1024]{2,0,1:T(8,128)} %bitcast.13), calls=%async_computation | async-start | bytes 262144 | tf_op jit(solution)/shard_map/all_to_all | solution.py:124
  123.4 7.8 %all-to-all-start.3 = ((s32[8,1,512]{2,1,0:T(1,128)}), s32[8,1,512]{2,1,0:T(1,128)S(1)}, u32[]{:S(2)}, u32[]{:S(2)}) async-start(s32[8,1,512]{2,1,0:T(1,128)} %reshape.251), calls=%async_computation.3 | async-start | bytes 32768 | tf_op jit(solution)/shard_map/all_to_all | solution.py:136
  132.1 3.1 %reshape.249 = f32[8,1,4096]{2,1,0:T(1,128)} reshape(f32[1024,4,8]{2,1,0:T(4,128)S(1)} %bitcast.98) | data formatting | bytes 262144
  136.0 3.4 %all-to-all-start.1 = ((f32[8,1,4096]{2,1,0:T(1,128)}), f32[8,1,4096]{2,1,0:T(1,128)S(1)}, u32[]{:S(2)}, u32[]{:S(2)}) async-start(f32[8,1,4096]{2,1,0:T(1,128)} %reshape.249), calls=%async_computation.1 | async-start | bytes 262144 | tf_op jit(solution)/shard_map/all_to_all | solution.py:123
  141.2 3.7 %all-to-all-done.1 = f32[8,1,4096]{2,1,0:T(1,128)S(1)} async-done(((f32[8,1,4096]{2,1,0:T(1,128)}), f32[8,1,4096]{2,1,0:T(1,128)S(1)}, u32[]{:S(2)}, u32[]{:S(2)}) %all-to-all-start.1) | async-done | bytes 131104 | tf_op jit(solution)/shard_map/all_to_all | solution.py:123
  149.7 22.6 %while.36 = (s32[]{:T(128)}, f32[8,4096]{1,0:T(8,128)S(1)}, f32[8,8,512]{2,0,1:T(8,128)S(1)}, s32[8,512]{1,0:T(8,128)S(1)}, s32[]{:T(128)}, /*index=5*/s32[]{:T(128)}) while((s32[]{:T(128)}, f32[8,4096]{1,0:T(8,128)S(1)}, f32[8,8,512]{2,0,1:T(8,128)S(1)}, s32[8,512]{1,0:T(8,128)S(1)}, s32[]{:T(128)}, /*index=5*/s32[]{:T(128)}) %tuple.113), condition=%wide.region_8.9_spmd.clone, body=%wide.region_7.8_spmd.clone.sunk | while | flops 203489280 | bytes 317527 | solution.py:167
  149.8 2.8 %fusion.133 = f32[8,4096]{1,0:T(8,128)S(1)} fusion(s32[512]{0:T(512)S(1)} %bitcast.121, f32[8,4096]{1,0:T(8,128)S(1)} %get-tuple-element.454, pred[]{:T(512)S(6)} %compare.13, f32[1,8,512]{2,0,1:T(1,128)S(1)} %constant_dynamic-slice_fusion.16), kind=kOutput, calls=%fused_computation.82.clone.1 | convolution fusion | flops 203489280 | bytes 280577 | tf_op jit(solution)/shard_map/while/body/eval_jaxpr/dot_general | solution.py:161
  152.6 2.8 %fusion.133 = f32[8,4096]{1,0:T(8,128)S(1)} fusion(s32[512]{0:T(512)S(1)} %bitcast.121, f32[8,4096]{1,0:T(8,128)S(1)} %get-tuple-element.454, pred[]{:T(512)S(6)} %compare.13, f32[1,8,512]{2,0,1:T(1,128)S(1)} %constant_dynamic-slice_fusion.16), kind=kOutput, calls=%fused_computation.82.clone.1 | convolution fusion | flops 203489280 | bytes 280577 | tf_op jit(solution)/shard_map/while/body/eval_jaxpr/dot_general | solution.py:161
  172.4 3.2 %collective-permute-start.8 = (f32[8,32,1]{2,1,0:T(8,128)S(1)}, f32[8,32,1]{2,1,0:T(8,128)S(1)}, u32[]{:S(2)}, u32[]{:S(2)}) collective-permute-start(f32[8,32,1]{2,1,0:T(8,128)S(1)} %get-tuple-element.275), channel_id=1, source_target_pairs={{0,8},{8,16},{16,24},{1,9},{9,17},{17,25},{2,10},{10,18},{18,26},{... | collective-permute-start | bytes 3080 | tf_op jit(solution)/shard_map/ppermute | solution.py:14
  178.2 4.3 %collective-permute-done.9 = f32[8,32,1]{2,1,0:T(8,128)S(1)} collective-permute-done((f32[8,32,1]{2,1,0:T(8,128)S(1)}, f32[8,32,1]{2,1,0:T(8,128)S(1)}, u32[]{:S(2)}, u32[]{:S(2)}) %collective-permute-start.9) | collective-permute-done | bytes 1056 | tf_op jit(solution)/shard_map/ppermute | solution.py:17
  183.9 3.0 %collective-permute-start.11 = (f32[8,1,130]{2,1,0:T(1,128)S(1)}, f32[8,1,130]{2,1,0:T(1,128)S(1)}, u32[]{:S(2)}, u32[]{:S(2)}) collective-permute-start(f32[8,1,130]{2,1,0:T(1,128)S(1)} %get-tuple-element.265), channel_id=1, source_target_pairs={{0,1},{1,2},{2,3},{3,4},{4,5},{5,6},{6,7},{8,9},{9,10},{10,11},{11... | collective-permute-start | bytes 12488 | tf_op jit(solution)/shard_map/ppermute | solution.py:14
  (168 shorter events, 69.2 us)
Async XLA Ops:
  0.6 27.2 %copy-start = (f32[8,8]{1,0:T(8,128)S(1)}, f32[8,8]{1,0:T(8,128)}, u32[]{:S(2)}) copy-start(f32[8,8]{1,0:T(8,128)} %param.16) | copy-start | bytes 772
  0.6 10.2 %copy-start.20 = (s32[2048,1]{0,1:T(1,128)S(1)}, s32[2048,1]{0,1:T(1,128)}, u32[]{:S(2)}) copy-start(s32[2048,1]{0,1:T(1,128)} %param.18) | copy-start | bytes 24580
  2.5 18.4 %copy-start.1 = (f32[16,16,128]{2,1,0:T(8,128)S(1)}, f32[16,16,128]{2,1,0:T(8,128)}, u32[]{:S(2)}) copy-start(f32[16,16,128]{2,1,0:T(8,128)} %param.15) | copy-start | bytes 393220
  3.3 17.5 %collective-permute-start = (f32[9,1,16,128]{3,0,2,1:T(8,128)S(1)}, f32[9,1,16,128]{3,0,2,1:T(8,128)S(1)}, u32[]{:S(2)}, u32[]{:S(2)}) collective-permute-start(f32[9,1,16,128]{3,0,2,1:T(8,128)S(1)} %get-tuple-element.256), channel_id=1, source_target_pairs={{0,8},{8,16},{16,24},{1,9},{9,17},{17,25},{2,10},{10,18},{18,26},{... | collective-permute-start | bytes 221192 | tf_op jit(solution)/shard_map/ppermute | solution.py:14
  8.2 15.4 %copy-start.21 = (s32[2048]{0:T(1024)S(1)}, s32[2048]{0:T(1024)}, u32[]{:S(2)}) copy-start(s32[2048]{0:T(1024)} %param.19) | copy-start | bytes 24580
  8.3 16.0 %copy-start.22 = (s32[2048]{0:T(1024)S(1)}, s32[2048]{0:T(1024)}, u32[]{:S(2)}) copy-start(s32[2048]{0:T(1024)} %param.20) | copy-start | bytes 24580
  8.3 12.6 %collective-permute-start.1 = (f32[9,1,16,128]{3,0,2,1:T(8,128)S(1)}, f32[9,1,16,128]{3,0,2,1:T(8,128)S(1)}, u32[]{:S(2)}, u32[]{:S(2)}) collective-permute-start(f32[9,1,16,128]{3,0,2,1:T(8,128)S(1)} %get-tuple-element.257), channel_id=1, source_target_pairs={{8,0},{16,8},{24,16},{9,1},{17,9},{25,17},{10,2},{18,10},{26,18},{... | collective-permute-start | bytes 221192 | tf_op jit(solution)/shard_map/ppermute | solution.py:17
  20.9 4.6 %collective-permute-start.2 = (f32[9,18,1,128]{3,0,2,1:T(8,128)S(1)}, f32[9,18,1,128]{3,0,2,1:T(8,128)S(1)}, u32[]{:S(2)}, u32[]{:S(2)}) collective-permute-start(f32[9,18,1,128]{3,0,2,1:T(8,128)S(1)} %get-tuple-element.253), channel_id=1, source_target_pairs={{0,1},{1,2},{2,3},{3,4},{4,5},{5,6},{6,7},{8,9},{9,10},{10,11},{11... | collective-permute-start | bytes 248840 | tf_op jit(solution)/shard_map/ppermute | solution.py:14
  22.4 4.8 %collective-permute-start.3 = (f32[9,18,1,128]{3,0,2,1:T(8,128)S(1)}, f32[9,18,1,128]{3,0,2,1:T(8,128)S(1)}, u32[]{:S(2)}, u32[]{:S(2)}) collective-permute-start(f32[9,18,1,128]{3,0,2,1:T(8,128)S(1)} %get-tuple-element.252), channel_id=1, source_target_pairs={{1,0},{2,1},{3,2},{4,3},{5,4},{6,5},{7,6},{9,8},{10,9},{11,10},{12... | collective-permute-start | bytes 248840 | tf_op jit(solution)/shard_map/ppermute | solution.py:17
  27.6 3.4 %copy-start.6 = (f32[16,16,128]{2,1,0:T(8,128)}, f32[16,16,128]{2,1,0:T(8,128)S(1)}, u32[]{:S(2)}) copy-start(f32[16,16,128]{2,1,0:T(8,128)S(1)} %get-tuple-element.266) | copy-start | bytes 393220
  27.6 3.4 %copy-start.8 = (f32[16,16,128]{2,1,0:T(8,128)}, f32[16,16,128]{2,1,0:T(8,128)S(1)}, u32[]{:S(2)}) copy-start(f32[16,16,128]{2,1,0:T(8,128)S(1)} %get-tuple-element.267) | copy-start | bytes 393220
  27.6 3.4 %copy-start.10 = (f32[16,16,128]{2,1,0:T(8,128)}, f32[16,16,128]{2,1,0:T(8,128)S(1)}, u32[]{:S(2)}) copy-start(f32[16,16,128]{2,1,0:T(8,128)S(1)} %get-tuple-element.268) | copy-start | bytes 393220
  31.1 16.2 %copy-start.7 = (f32[16,16,128]{2,1,0:T(8,128)S(1)}, f32[16,16,128]{2,1,0:T(8,128)}, u32[]{:S(2)}) copy-start(f32[16,16,128]{2,1,0:T(8,128)} %copy-done.6) | copy-start | bytes 393220
  31.1 16.2 %copy-start.9 = (f32[16,16,128]{2,1,0:T(8,128)S(1)}, f32[16,16,128]{2,1,0:T(8,128)}, u32[]{:S(2)}) copy-start(f32[16,16,128]{2,1,0:T(8,128)} %copy-done.8) | copy-start | bytes 393220
  31.1 16.1 %copy-start.11 = (f32[16,16,128]{2,1,0:T(8,128)S(1)}, f32[16,16,128]{2,1,0:T(8,128)}, u32[]{:S(2)}) copy-start(f32[16,16,128]{2,1,0:T(8,128)} %copy-done.10) | copy-start | bytes 393220
  31.1 16.1 %copy-start.13 = (f32[16,16,128]{2,1,0:T(8,128)S(1)}, f32[16,16,128]{2,1,0:T(8,128)}, u32[]{:S(2)}) copy-start(f32[16,16,128]{2,1,0:T(8,128)} %copy-done.12) | copy-start | bytes 393220
  31.1 16.1 %copy-start.15 = (f32[16,16,128]{2,1,0:T(8,128)S(1)}, f32[16,16,128]{2,1,0:T(8,128)}, u32[]{:S(2)}) copy-start(f32[16,16,128]{2,1,0:T(8,128)} %copy-done.14) | copy-start | bytes 393220
  31.1 16.1 %copy-start.17 = (f32[16,16,128]{2,1,0:T(8,128)S(1)}, f32[16,16,128]{2,1,0:T(8,128)}, u32[]{:S(2)}) copy-start(f32[16,16,128]{2,1,0:T(8,128)} %copy-done.16) | copy-start | bytes 393220
  31.1 7.4 %collective-permute-start.4 = (f32[8,1,16,128]{3,0,2,1:T(8,128)S(1)}, f32[8,1,16,128]{3,0,2,1:T(8,128)S(1)}, u32[]{:S(2)}, u32[]{:S(2)}) collective-permute-start(f32[8,1,16,128]{3,0,2,1:T(8,128)S(1)} %get-tuple-element.261), channel_id=1, source_target_pairs={{8,0},{16,8},{24,16},{9,1},{17,9},{25,17},{10,2},{18,10},{26,18},{... | collective-permute-start | bytes 196616 | tf_op jit(solution)/shard_map/ppermute | solution.py:17
  32.6 7.1 %collective-permute-start.5 = (f32[8,1,16,128]{3,0,2,1:T(8,128)S(1)}, f32[8,1,16,128]{3,0,2,1:T(8,128)S(1)}, u32[]{:S(2)}, u32[]{:S(2)}) collective-permute-start(f32[8,1,16,128]{3,0,2,1:T(8,128)S(1)} %get-tuple-element.260), channel_id=1, source_target_pairs={{0,8},{8,16},{16,24},{1,9},{9,17},{17,25},{2,10},{10,18},{18,26},{... | collective-permute-start | bytes 196616 | tf_op jit(solution)/shard_map/ppermute | solution.py:14
  39.6 7.0 %collective-permute-start.6 = (f32[8,18,1,128]{3,0,2,1:T(8,128)S(1)}, f32[8,18,1,128]{3,0,2,1:T(8,128)S(1)}, u32[]{:S(2)}, u32[]{:S(2)}) collective-permute-start(f32[8,18,1,128]{3,0,2,1:T(8,128)S(1)} %get-tuple-element.254), channel_id=1, source_target_pairs={{1,0},{2,1},{3,2},{4,3},{5,4},{6,5},{7,6},{9,8},{10,9},{11,10},{12... | collective-permute-start | bytes 221192 | tf_op jit(solution)/shard_map/ppermute | solution.py:17
  40.9 6.3 %collective-permute-start.7 = (f32[8,18,1,128]{3,0,2,1:T(8,128)S(1)}, f32[8,18,1,128]{3,0,2,1:T(8,128)S(1)}, u32[]{:S(2)}, u32[]{:S(2)}) collective-permute-start(f32[8,18,1,128]{3,0,2,1:T(8,128)S(1)} %get-tuple-element.255), channel_id=1, source_target_pairs={{0,1},{1,2},{2,3},{3,4},{4,5},{5,6},{6,7},{8,9},{9,10},{10,11},{11... | collective-permute-start | bytes 221192 | tf_op jit(solution)/shard_map/ppermute | solution.py:14
  50.1 37.7 %copy-start.19 = (f32[9,4096]{1,0:T(8,128)S(1)}, f32[9,4096]{1,0:T(8,128)}, u32[]{:S(2)}) copy-start(f32[9,4096]{1,0:T(8,128)} %custom-call) | copy-start | bytes 442372
  102.4 11.1 %all-to-all-start.2 = ((s32[1,4,1024]{2,0,1:T(1,128)}), s32[1,4,1024]{2,0,1:T(1,128)S(1)}, u32[]{:S(2)}, u32[]{:S(2)}) async-start(s32[1,4,1024]{2,0,1:T(1,128)} %bitcast.15), calls=%async_computation.2 | async-start | bytes 32768 | tf_op jit(solution)/shard_map/all_to_all | solution.py:137
  113.5 9.9 %all-to-all-start = ((f32[8,4,1024]{2,0,1:T(8,128)}), f32[8,4,1024]{2,0,1:T(8,128)S(1)}, u32[]{:S(2)}, u32[]{:S(2)}) async-start(f32[8,4,1024]{2,0,1:T(8,128)} %bitcast.13), calls=%async_computation | async-start | bytes 262144 | tf_op jit(solution)/shard_map/all_to_all | solution.py:124
  123.4 12.6 %all-to-all-start.3 = ((s32[8,1,512]{2,1,0:T(1,128)}), s32[8,1,512]{2,1,0:T(1,128)S(1)}, u32[]{:S(2)}, u32[]{:S(2)}) async-start(s32[8,1,512]{2,1,0:T(1,128)} %reshape.251), calls=%async_computation.3 | async-start | bytes 32768 | tf_op jit(solution)/shard_map/all_to_all | solution.py:136
  136.0 8.9 %all-to-all-start.1 = ((f32[8,1,4096]{2,1,0:T(1,128)}), f32[8,1,4096]{2,1,0:T(1,128)S(1)}, u32[]{:S(2)}, u32[]{:S(2)}) async-start(f32[8,1,4096]{2,1,0:T(1,128)} %reshape.249), calls=%async_computation.1 | async-start | bytes 262144 | tf_op jit(solution)/shard_map/all_to_all | solution.py:123
  149.7 22.6 %copy-start.5 = (f32[8,32,128]{2,1,0:T(8,128)S(1)}, f32[8,32,128]{2,1,0:T(8,128)}, u32[]{:S(2)}) copy-start(f32[8,32,128]{2,1,0:T(8,128)} %param.17) | copy-start | bytes 393220
  172.4 5.7 %collective-permute-start.8 = (f32[8,32,1]{2,1,0:T(8,128)S(1)}, f32[8,32,1]{2,1,0:T(8,128)S(1)}, u32[]{:S(2)}, u32[]{:S(2)}) collective-permute-start(f32[8,32,1]{2,1,0:T(8,128)S(1)} %get-tuple-element.275), channel_id=1, source_target_pairs={{0,8},{8,16},{16,24},{1,9},{9,17},{17,25},{2,10},{10,18},{18,26},{... | collective-permute-start | bytes 3080 | tf_op jit(solution)/shard_map/ppermute | solution.py:14
  175.6 6.9 %collective-permute-start.9 = (f32[8,32,1]{2,1,0:T(8,128)S(1)}, f32[8,32,1]{2,1,0:T(8,128)S(1)}, u32[]{:S(2)}, u32[]{:S(2)}) collective-permute-start(f32[8,32,1]{2,1,0:T(8,128)S(1)} %get-tuple-element.274), channel_id=1, source_target_pairs={{8,0},{16,8},{24,16},{9,1},{17,9},{25,17},{10,2},{18,10},{26,18},{... | collective-permute-start | bytes 3080 | tf_op jit(solution)/shard_map/ppermute | solution.py:17
  182.6 5.5 %collective-permute-start.10 = (f32[8,1,130]{2,1,0:T(1,128)S(1)}, f32[8,1,130]{2,1,0:T(1,128)S(1)}, u32[]{:S(2)}, u32[]{:S(2)}) collective-permute-start(f32[8,1,130]{2,1,0:T(1,128)S(1)} %get-tuple-element.264), channel_id=1, source_target_pairs={{1,0},{2,1},{3,2},{4,3},{5,4},{6,5},{7,6},{9,8},{10,9},{11,10},{12... | collective-permute-start | bytes 12488 | tf_op jit(solution)/shard_map/ppermute | solution.py:17
  183.9 4.2 %collective-permute-start.11 = (f32[8,1,130]{2,1,0:T(1,128)S(1)}, f32[8,1,130]{2,1,0:T(1,128)S(1)}, u32[]{:S(2)}, u32[]{:S(2)}) collective-permute-start(f32[8,1,130]{2,1,0:T(1,128)S(1)} %get-tuple-element.265), channel_id=1, source_target_pairs={{0,1},{1,2},{2,3},{3,4},{4,5},{5,6},{6,7},{8,9},{9,10},{10,11},{11... | collective-permute-start | bytes 12488 | tf_op jit(solution)/shard_map/ppermute | solution.py:14
  (7 other events, 16.5 us)
where the time goes:
time: 190 us; the launch traced here: 189 us
  matrix products  52.7 us (28%)
  starting transfers between devices  51.3 us (27%)
  other arithmetic  33.9 us (18%)
  local copies, waits for them, and re-layouts  28.4 us (15%)
  waiting for transfers between devices  21 us (11%)
    ppermute x6, starting transfers between devices, extended(): lax.ppermute(lax.slice_in_dim(block, block.shape[dim] - width, None, axis...  23.2 us
    dot_general x8, matrix products, land(): jnp.dot(vals, placing, precision=lax.Precision.HIGHEST, preferred_element...  22.1 us
    dot_general x4, other arithmetic, interpolate(): lax.dot_general(shell, table, (((1,), (1,)), ((), ())), precision=lax.Pre...  16.7 us
    dot_general x4, matrix products, interpolate(): lax.dot_general(shell, table, (((1,), (1,)), ((), ())), precision=lax.Pre...  14.6 us
    unnamed x54, local copies, waits for them, and re-layouts  11.3 us
    dot_general x4, matrix products, pack(): jnp.dot(rows, placing, precision=lax.Precision.HIGHEST, preferred_element...  11.1 us
    another operation x3, other arithmetic  9.41 us
    ppermute x6, starting transfers between devices, extended(): lax.ppermute(lax.slice_in_dim(block, 0, width, axis=dim), axis, backward)  7.88 us
  transfers between devices with their start and end apart: 16, of which 9 were waited for; matrix products, arithmetic and copies ran while one was open for 13% of the time, Pallas kernels for 0%

commit v1 on v0

v1 whole, which is shorter than its diff:
```python
import functools

import jax
import jax.numpy as jnp
from jax import lax
from jax.experimental import pallas as pl
from jax.experimental.pallas import tpu as pltpu
from jax.sharding import PartitionSpec as P

SH = 8
F32 = jnp.float32
BF16 = jnp.bfloat16
MESH = pl.DeviceIdType.MESH
LANES = 128
GROUP = 8
LAND = 4
NPAR = 5


def iota(shape, dim):
    return lax.broadcasted_iota(jnp.int32, shape, dim)


def split(x):
    hi = x.astype(BF16)
    return hi, (x - hi.astype(F32)).astype(BF16)


def dot_t(a, b):
    return lax.dot_general(a, b, (((1,), (1,)), ((), ())), preferred_element_type=F32)


def apply_step(c, near, kc, knear, mix):
    lane = iota(kc.shape, 1)
    last = kc.shape[1] - 1
    ks = [0.075 * (kc + kn) for kn in knear]
    kl = 0.075 * (kc + jnp.where(lane == 0, 0.0, pltpu.roll(kc, 1, 1)))
    kr = 0.075 * (kc + jnp.where(lane == last, 0.0, pltpu.roll(kc, last, 1)))
    diag = 1.0 - (((ks[0] + ks[1]) + (ks[2] + ks[3])) + (kl + kr))
    kl = jnp.where(lane == 0, 0.0, kl)
    kr = jnp.where(lane == last, 0.0, kr)
    total = diag[None] * c
    for k, u in zip(ks, near):
        total = total + k[None] * u
    total = total + kl[None] * pltpu.roll(c, 1, 2) + kr[None] * pltpu.roll(c, last, 2)
    out = []
    for g in range(c.shape[0]):
        row = total[g]
        for f in range(c.shape[0]):
            row = row + (0.3 * mix[g, f]) * c[f]
        out.append(row)
    return out


def shift_rows(c, low, high):
    n = c.shape[1]
    row = iota(c.shape, 1)
    down = jnp.where(row == 0, low, pltpu.roll(c, 1, 1))
    up = jnp.where(row == n - 1, high, pltpu.roll(c, n - 1, 1))
    return down, up


def kernel(
    n_lat, n_lon, corona, kappa, mix, helio, owner, dest, base, frac, stepped, face,
    ue, sp, pleft, pright, q2, cs, cr, first, fleft, fright, st, pk, ds, rd, vs, rv,
    shell, hs, hr, ts, tr, acc, load_sem, halo_send, halo_recv, out_sem,
    dest_send, dest_recv, val_send, val_recv, face_send, face_recv,
):
    n_dev = n_lat * n_lon
    fields = corona.shape[0]
    tt, pp = corona.shape[1], corona.shape[2]
    count = owner.shape[1]
    lat, lon = lax.axis_index("lat"), lax.axis_index("lon")
    me = lat * n_lon + lon

    loads = [
        pltpu.make_async_copy(corona, ue.at[0:fields, 2 : 2 + tt], load_sem.at[0]),
        pltpu.make_async_copy(kappa, ue.at[fields, 2 : 2 + tt], load_sem.at[1]),
    ]
    for copy in loads:
        copy.start()

    barrier = pltpu.get_barrier_semaphore()

    def greet(i, carry):
        o = lax.rem(me + i, n_dev)
        pl.semaphore_signal(
            barrier, inc=1, device_id=(lax.div(o, n_lon), lax.rem(o, n_lon)), device_id_type=MESH
        )
        return carry

    lax.fori_loop(1, n_dev, greet, 0)
    for copy in loads:
        copy.wait()

    for j, p in enumerate((0, 1, pp - 2, pp - 1)):
        sp[j] = ue[:, 2 : 2 + tt, p, :]
    corners = [(1, 1), (1, -1), (-1, 1), (-1, -1)]
    for k, (a, b) in enumerate(corners):
        t, p = (2 + tt - 1 if a > 0 else 2), (pp - 1 if b > 0 else 0)
        for f in range(fields + 1):
            cs[k, f : f + 1, :] = ue[f, t, p : p + 1, :]

    moves = [
        ((1, 0), ue.at[:, tt : tt + 2], ue.at[:, 0:2]),
        ((-1, 0), ue.at[:, 2:4], ue.at[:, tt + 2 : tt + 4]),
        ((0, 1), sp.at[3], pleft.at[:, 8 : 8 + tt]),
        ((0, 1), sp.at[2], q2.at[0]),
        ((0, -1), sp.at[0], pright.at[:, 8 : 8 + tt]),
        ((0, -1), sp.at[1], q2.at[1]),
    ] + [(ab, cs.at[k], cr.at[k]) for k, ab in enumerate(corners)]

    def inside(a, b):
        ok = lat >= 0
        if a > 0:
            ok = ok & (lat < n_lat - 1)
        if a < 0:
            ok = ok & (lat > 0)
        if b > 0:
            ok = ok & (lon < n_lon - 1)
        if b < 0:
            ok = ok & (lon > 0)
        return ok

    def remote(a, b, src, dst, send, recv):
        return pltpu.make_async_remote_copy(
            src_ref=src, dst_ref=dst, send_sem=send, recv_sem=recv,
            device_id=(lat + a, lon + b), device_id_type=MESH,
        )

    pl.semaphore_wait(barrier, n_dev - 1)
    for k, ((a, b), src, dst) in enumerate(moves):

        @pl.when(inside(a, b))
        def _(k=k, a=a, b=b, src=src, dst=dst):
            remote(a, b, src, dst, halo_send.at[k], halo_recv.at[k]).start()

        @pl.when(jnp.logical_not(inside(-a, -b)))
        def _(dst=dst):
            dst[...] = jnp.zeros(dst.shape, F32)

    own = owner[...]
    upper = (iota((LANES, LANES), 0) < iota((LANES, LANES), 1)).astype(F32).astype(BF16)
    carry = jnp.zeros((n_dev, 1), F32)
    ranks = []
    for blk in range(count // LANES):
        hit = jnp.where(
            iota((n_dev, LANES), 0) == own[:, blk * LANES : (blk + 1) * LANES], 1.0, 0.0
        )
        before = jnp.dot(hit.astype(BF16), upper, preferred_element_type=F32) + carry
        ranks.append(jnp.sum(hit * before, axis=0, keepdims=True))
        carry = carry + jnp.sum(hit, axis=1, keepdims=True)
    rank = jnp.concatenate(ranks, axis=1).astype(jnp.int32)
    rank_hot = jnp.where(iota((LANES, count), 0) == rank, 1.0, 0.0).astype(BF16)
    rows = [base[...].astype(F32)] + [frac[i : i + 1, :] for i in range(3)]
    rows.append((dest[...] + 1).astype(F32))
    pieces = []
    for row in rows:
        hi = row.astype(BF16).astype(F32)
        pieces += [hi, row - hi]
    chunk = 32

    def place(g, carry):
        mask = iota((chunk, count), 0) + g * chunk == own
        left = jnp.concatenate([jnp.where(mask, x, 0.0).astype(BF16) for x in pieces], axis=0)
        got = dot_t(left, rank_hot)
        for q in range(NPAR):
            val = got[2 * q * chunk : (2 * q + 1) * chunk] + got[(2 * q + 1) * chunk : (2 * q + 2) * chunk]
            for oc in range(chunk // GROUP):
                pk[g * (chunk // GROUP) + oc, q] = val[oc * GROUP : (oc + 1) * GROUP]
            if q == NPAR - 1:
                for o in range(chunk):
                    ds[g * chunk + o] = val[o : o + 1]
        return carry

    lax.fori_loop(0, n_dev // chunk, place, 0)

    def send_to(o, src, dst, send, recv):
        return pltpu.make_async_remote_copy(
            src_ref=src, dst_ref=dst, send_sem=send, recv_sem=recv,
            device_id=(lax.div(o, n_lon), lax.rem(o, n_lon)), device_id_type=MESH,
        )

    def send_dest(i, carry):
        o = lax.rem(me + i, n_dev)
        send_to(o, ds.at[o], rd.at[me], dest_send, dest_recv).start()
        return carry

    lax.fori_loop(1, n_dev, send_dest, 0)
    rd[me] = ds[me]

    for k, ((a, b), src, dst) in enumerate(moves):

        @pl.when(inside(-a, -b))
        def _(k=k, a=a, b=b, src=src, dst=dst):
            remote(-a, -b, src, dst, halo_send.at[k], halo_recv.at[k]).wait_recv()

    for k, (a, b) in enumerate(corners):
        side = pleft if b > 0 else pright
        row = 7 if a > 0 else 8 + tt
        for f in range(fields + 1):
            side[f, row : row + 1, :] = cr[k, f : f + 1, :]

    def first_row(i, carry):
        c = ue[:, i + 1]
        low, high = shift_rows(c, pleft[:, pl.ds(7 + i, 1), :], pright[:, pl.ds(7 + i, 1), :])
        up, down = ue[:, i], ue[:, i + 2]
        out = apply_step(
            c[:fields], [x[:fields] for x in (up, down, low, high)],
            c[fields], [x[fields] for x in (up, down, low, high)], mix,
        )
        off = ((i == 0) & (lat == 0)) | ((i == tt + 1) & (lat == n_lat - 1))
        keep = jnp.where(off, 0.0, 1.0)
        for g in range(fields):
            first[g, i] = out[g] * keep
        return carry

    lax.fori_loop(0, tt + 2, first_row, 0)
    for side, outer, inner, into, ok in (
        (pleft, q2.at[0], sp.at[0], fleft, lon > 0),
        (pright, q2.at[1], sp.at[3], fright, lon < n_lon - 1),
    ):
        near = [side[:, 7 : 7 + tt, :], side[:, 9 : 9 + tt, :], outer[...], inner[...]]
        c = side[:, 8 : 8 + tt, :]
        out = apply_step(c[:fields], [x[:fields] for x in near], c[fields], [x[fields] for x in near], mix)
        keep = jnp.where(ok, 1.0, 0.0)
        for g in range(fields):
            into[g] = out[g] * keep

    def second_row(t, carry):
        c = first[:, t + 1]
        low, high = shift_rows(c, fleft[:, pl.ds(t, 1), :], fright[:, pl.ds(t, 1), :])
        kc = ue[fields:, t + 2]
        klow, khigh = shift_rows(
            kc, pleft[fields:, pl.ds(8 + t, 1), :], pright[fields:, pl.ds(8 + t, 1), :]
        )
        out = apply_step(
            c, [first[:, t], first[:, t + 2], low, high],
            kc[0], [ue[fields, t + 1], ue[fields, t + 3], klow[0], khigh[0]], mix,
        )
        for g in range(fields):
            st[g, t] = out[g]
        return carry

    lax.fori_loop(0, tt, second_row, 0)
    write = pltpu.make_async_copy(st, stepped, out_sem)
    write.start()

    n_r = st.shape[3]

    def shell_row(t, carry):
        lane = iota((fields, LANES), 1)
        row = jnp.zeros((fields, LANES), F32)
        for p in range(pp):
            x = pltpu.roll(st[:, t, p, :], (p * SH + SH) % n_r, 1)
            row = jnp.where((lane >= p * SH) & (lane < (p + 1) * SH), x, row)
        shell[t] = row
        return carry

    lax.fori_loop(0, tt, shell_row, 0)
    s_hi, s_lo = split(shell[...].reshape(tt * fields, LANES))
    left = jnp.concatenate([s_hi, s_hi, s_lo], axis=1)
    groups = n_dev // GROUP
    wide = GROUP * LANES

    def values(i, carry):
        g = lax.rem(lax.div(me, GROUP) + i, groups)
        par = [
            jnp.concatenate([pk[g, q, k : k + 1, :] for k in range(GROUP)], axis=1)
            for q in range(NPAR - 1)
        ]
        cell = par[0].astype(jnp.int32)
        t0, p0, r0 = cell >> 7, (cell >> 3) & 15, cell & 7
        fx, fy, fz = par[1:]

        def weights(n, at, fr):
            idx = iota((n, wide), 0) - at
            return jnp.where(idx == 0, 1.0 - fr, jnp.where(idx == 1, fr, 0.0))

        wa, wb, wc = weights(tt, t0, fx), weights(pp, p0, fy), weights(SH, r0, fz)
        table = (wb[:, None, :] * wc[None]).reshape(pp * SH, wide)
        hi, lo = split(table)
        got = jnp.dot(left, jnp.concatenate([hi, lo, hi], axis=0), preferred_element_type=F32)
        val = jnp.sum(got.reshape(tt, fields, wide) * wa[:, None, :], axis=0)
        for k in range(GROUP):
            vs[g * GROUP + k] = val[:, k * LANES : (k + 1) * LANES]
        for k in range(GROUP):
            o = g * GROUP + k

            @pl.when(o != me)
            def _(o=o):
                send_to(o, vs.at[o], rv.at[me], val_send, val_recv).start()

        return carry

    lax.fori_loop(0, groups, values, 0)
    rv[me] = vs[me]

    other = lax.rem(me + 1, n_dev)
    all_dest = send_to(other, ds.at[0 : n_dev - 1], rd.at[0 : n_dev - 1], dest_send, dest_recv)
    all_vals = send_to(other, vs.at[0 : n_dev - 1], rv.at[0 : n_dev - 1], val_send, val_recv)
    all_dest.wait_recv()
    all_vals.wait_recv()

    face_p, face_t = helio.shape[1], helio.shape[2]
    acc[...] = jnp.zeros(acc.shape, F32)

    def land(i, carry):
        cell = jnp.concatenate([rd[i * LAND + k] for k in range(LAND)], axis=1).astype(jnp.int32) - 1
        val = jnp.concatenate([rv[i * LAND + k] for k in range(LAND)], axis=1)
        hi = val.astype(BF16).astype(F32)
        on_p = iota((face_p, LAND * LANES), 0) == (cell >> 7)
        on_t = jnp.where(iota((face_t, LAND * LANES), 0) == (cell & 127), 1.0, 0.0).astype(BF16)
        spread = jnp.concatenate(
            [jnp.where(on_p, x[f : f + 1], 0.0).astype(BF16) for x in (hi, val - hi) for f in range(fields)],
            axis=0,
        )
        acc[...] += dot_t(spread, on_t)
        return carry

    lax.fori_loop(0, n_dev // LAND, land, 0)
    half = fields * face_p
    flat = helio[...].reshape(half, face_t) + (acc[0:half] + acc[half:])
    coupled = flat.reshape(fields, face_p, face_t)

    for f in range(fields):
        hs[0, f : f + 1, :] = coupled[f, 0:1, :]
        hs[1, f : f + 1, :] = coupled[f, face_p - 1 : face_p, :]
    row8, lane8 = iota((8, face_t), 0), iota((8, face_t), 1)
    pick = jnp.where(
        ((row8 == 0) & (lane8 == 0)) | ((row8 == 1) & (lane8 == face_t - 1)), 1.0, 0.0
    )
    ts[...] = lax.dot_general(
        pick, flat, (((1,), (1,)), ((), ())), precision=lax.Precision.HIGHEST, preferred_element_type=F32
    )
    edges = [
        ((0, 1), hs.at[1], hr.at[0]),
        ((0, -1), hs.at[0], hr.at[1]),
        ((1, 0), ts, tr.at[0]),
        ((-1, 0), ts, tr.at[1]),
    ]
    for k, ((a, b), src, dst) in enumerate(edges):

        @pl.when(inside(a, b))
        def _(k=k, a=a, b=b, src=src, dst=dst):
            remote(a, b, src, dst, face_send.at[k], face_recv.at[k]).start()

        @pl.when(jnp.logical_not(inside(-a, -b)))
        def _(dst=dst):
            dst[...] = jnp.zeros(dst.shape, F32)

    lane3 = iota(coupled.shape, 2)
    inner = (
        jnp.where(lane3 == 0, 0.0, pltpu.roll(coupled, 1, 2))
        + jnp.where(lane3 == face_t - 1, 0.0, pltpu.roll(coupled, face_t - 1, 2))
        - 4.0 * coupled
    )
    for k, ((a, b), src, dst) in enumerate(edges):

        @pl.when(inside(-a, -b))
        def _(k=k, a=a, b=b, src=src, dst=dst):
            remote(-a, -b, src, dst, face_send.at[k], face_recv.at[k]).wait_recv()

    lows = jnp.concatenate([hr[0, f : f + 1, :][None] for f in range(fields)], axis=0)
    highs = jnp.concatenate([hr[1, f : f + 1, :][None] for f in range(fields)], axis=0)
    down, up = shift_rows(coupled, lows, highs)
    put_low = jnp.where((row8 == 1) & (lane8 == 0), 1.0, 0.0)
    put_high = jnp.where((row8 == 0) & (lane8 == face_t - 1), 1.0, 0.0)
    both = jnp.concatenate([tr[0], tr[1]], axis=0)
    sides = lax.dot_general(
        both, jnp.concatenate([put_low, put_high], axis=0), (((0,), (0,)), ((), ())),
        precision=lax.Precision.HIGHEST, preferred_element_type=F32,
    ).reshape(coupled.shape)
    face[...] = coupled + 0.2 * (inner + (down + up) + sides)

    for k, ((a, b), src, dst) in enumerate(moves):

        @pl.when(inside(a, b))
        def _(k=k, a=a, b=b, src=src, dst=dst):
            remote(a, b, src, dst, halo_send.at[k], halo_recv.at[k]).wait_send()

    for k, ((a, b), src, dst) in enumerate(edges):

        @pl.when(inside(a, b))
        def _(k=k, a=a, b=b, src=src, dst=dst):
            remote(a, b, src, dst, face_send.at[k], face_recv.at[k]).wait_send()

    all_dest.wait_send()
    all_vals.wait_send()
    write.wait()


def body(corona, kappa, mixing, helio_prev, owner, dest_cell, corner_base, fractions):
    n_lat, n_lon = lax.axis_size("lat"), lax.axis_size("lon")
    n_dev = n_lat * n_lon
    fields, tt, pp, n_r = corona.shape
    count = corner_base.shape[0]
    face_p, face_t = helio_prev.shape[1:]
    ext = fields + 1
    vmem = pl.BlockSpec(memory_space=pltpu.VMEM)
    hbm = pl.BlockSpec(memory_space=pl.ANY)
    sem = pltpu.SemaphoreType.DMA
    v = lambda *shape: pltpu.VMEM(shape, F32)
    return pl.pallas_call(
        functools.partial(kernel, n_lat, n_lon),
        out_shape=(
            jax.ShapeDtypeStruct(corona.shape, F32),
            jax.ShapeDtypeStruct(helio_prev.shape, F32),
        ),
        in_specs=[hbm, hbm, pl.BlockSpec(memory_space=pltpu.SMEM)] + [vmem] * 5,
        out_specs=(hbm, vmem),
        scratch_shapes=[
            v(ext, tt + 4, pp, n_r),
            v(4, ext, tt, n_r),
            v(ext, tt + 16, n_r),
            v(ext, tt + 16, n_r),
            v(2, ext, tt, n_r),
            v(4, 16, n_r),
            v(4, 16, n_r),
            v(fields, tt + 2, pp, n_r),
            v(fields, tt, n_r),
            v(fields, tt, n_r),
            v(fields, tt, pp, n_r),
            v(n_dev // GROUP, NPAR, GROUP, LANES),
            v(n_dev, 1, LANES),
            v(n_dev, 1, LANES),
            v(n_dev, fields, LANES),
            v(n_dev, fields, LANES),
            v(tt, fields, LANES),
            v(2, fields, face_t),
            v(2, fields, face_t),
            v(8, fields * face_p),
            v(2, 8, fields * face_p),
            v(2 * fields * face_p, face_t),
            sem((2,)), sem((10,)), sem((10,)), sem,
            sem, sem, sem, sem, sem((4,)), sem((4,)),
        ],
        compiler_params=pltpu.CompilerParams(
            collective_id=0, has_side_effects=True, vmem_limit_bytes=48 * 1024 * 1024
        ),
        name="corona_helio",
    )(
        corona, kappa, mixing, helio_prev, owner.reshape(1, count), dest_cell.reshape(1, count),
        corner_base.reshape(1, count), fractions,
    )


def solution(mesh):
    return jax.shard_map(
        body,
        mesh=mesh,
        in_specs=(
            P(None, "lat", "lon", None),
            P("lat", "lon", None),
            P(),
            P(None, "lon", "lat"),
            P(("lat", "lon"), None),
            P(("lat", "lon")),
            P(("lat", "lon")),
            P(None, ("lat", "lon")),
        ),
        out_specs=(P(None, "lat", "lon", None), P(None, "lon", "lat")),
        check_vma=False,
    )
```

time: 190 us -> 40.7 us (0.21)
  matrix products: 52.7 us -> 0 us
  starting transfers between devices: 51.3 us -> 0 us
  other arithmetic: 33.9 us -> 0 us
  Pallas kernels: 0 us -> 31.4 us
  waiting for transfers between devices: 21 us -> 0 us
  local copies, waits for them, and re-layouts: 28.4 us -> 8.19 us
    dot_general x18 -> x0, matrix products: 52.7 us -> none  [the longest x8 22.1 us: land(): jnp.dot(vals, placing, precision=lax.Precision.HIGHEST, preferred_element...]
    pallas_call x0 -> x1, Pallas kernels: none -> 31.4 us  [body(): pl.pallas_call(functools.partial(kernel, n_lat, n_lon), out_shape=(jax.Sh...]
    ppermute x12 -> x0, starting transfers between devices: 31.1 us -> none  [the longest x6 23.2 us: extended(): lax.ppermute(lax.slice_in_dim(block, block.shape[dim] - width, None, axis...]
    all_to_all x4 -> x0, starting transfers between devices: 20.3 us -> none  [the longest x1 7.81 us: body(): lax.all_to_all(lax.all_to_all(send_dest.reshape(1, n_lat, n_lon * slots_e...]
    dot_general x4 -> x0, other arithmetic: 16.7 us -> none  [interpolate(): lax.dot_general(shell, table, (((1,), (1,)), ((), ())), precision=lax.Pre...]
    all_to_all x4 -> x0, waiting for transfers between devices: 12.1 us -> none  [the longest x1 4.95 us: body(): lax.all_to_all(send_dest.reshape(1, n_lat, n_lon * slots_each), 'lat', sp...]
    another operation x3 -> x0, other arithmetic: 9.41 us -> none
    ppermute x12 -> x0, waiting for transfers between devices: 8.92 us -> none  [the longest x6 6.03 us: extended(): lax.ppermute(lax.slice_in_dim(block, 0, width, axis=dim), axis, backward)]
  transfers between devices with their start and end apart: 16 -> 0, of which waited for: 9 -> 0; matrix products, arithmetic and copies ran while one was open for 13% -> 0% of each run, Pallas kernels for 0% -> 0%
where the time goes in v1:
time: 40.7 us; the launch traced here: 40.3 us
  Pallas kernels  31.4 us (77%)
  local copies, waits for them, and re-layouts  8.19 us (20%)
  between operations  0.66 us (2%)
    pallas_call x1, Pallas kernels, body(): pl.pallas_call(functools.partial(kernel, n_lat, n_lon), out_shape=(jax.Sh...  31.4 us
    unnamed x18, local copies, waits for them, and re-layouts  8.19 us

profile of v1, /device:TPU:0, one launch (start us, length us, event | category | flops | bytes accessed | tf_op | source)
XLA Modules:
  0.0 40.3 jit_solution(8245589134874564356)
XLA Ops:
  0.6 0.0 copy-start.7
  0.6 0.7 %copy-done.7 = f32[8,8]{1,0:T(8,128)S(1)} copy-done((f32[8,8]{1,0:T(8,128)S(1)}, f32[8,8]{1,0:T(8,128)}, u32[]{:S(2)}) %copy-start.7) | copy-done | bytes 280
  1.3 0.0 copy-start
  1.3 1.2 %copy-done = f32[8,16,16,128]{3,2,1,0:T(8,128)S(1)} copy-done((f32[8,16,16,128]{3,2,1,0:T(8,128)S(1)}, f32[8,16,16,128]{3,2,1,0:T(8,128)}, u32[]{:S(2)}) %copy-start) | copy-done | bytes 1048600
  2.5 0.0 copy-start.1
  2.5 0.9 %copy-done.1 = f32[16,16,128]{2,1,0:T(8,128)S(1)} copy-done((f32[16,16,128]{2,1,0:T(8,128)S(1)}, f32[16,16,128]{2,1,0:T(8,128)}, u32[]{:S(2)}) %copy-start.1) | copy-done | bytes 131096
  3.5 0.0 copy-start.2
  3.5 0.9 %copy-done.2 = f32[8,32,128]{2,1,0:T(8,128)S(1)} copy-done((f32[8,32,128]{2,1,0:T(8,128)S(1)}, f32[8,32,128]{2,1,0:T(8,128)}, u32[]{:S(2)}) %copy-start.2) | copy-done | bytes 131096
  4.4 0.0 copy-start.3
  4.4 0.8 %copy-done.3 = f32[3,2048]{1,0:T(4,128)S(1)} copy-done((f32[3,2048]{1,0:T(4,128)S(1)}, f32[3,2048]{1,0:T(4,128)}, u32[]{:S(2)}) %copy-start.3) | copy-done | bytes 24600
  5.1 0.0 copy-start.4
  5.1 0.7 %copy-done.4 = s32[2048,1]{0,1:T(1,128)S(1)} copy-done((s32[2048,1]{0,1:T(1,128)S(1)}, s32[2048,1]{0,1:T(1,128)}, u32[]{:S(2)}) %copy-start.4) | copy-done | bytes 8216
  5.8 0.0 copy-start.5
  5.8 0.7 %copy-done.5 = s32[2048]{0:T(1024)S(1)} copy-done((s32[2048]{0:T(1024)S(1)}, s32[2048]{0:T(1024)}, u32[]{:S(2)}) %copy-start.5) | copy-done | bytes 8216
  6.5 0.0 copy-start.6
  6.5 0.7 %copy-done.6 = s32[2048]{0:T(1024)S(1)} copy-done((s32[2048]{0:T(1024)S(1)}, s32[2048]{0:T(1024)}, u32[]{:S(2)}) %copy-start.6) | copy-done | bytes 8216
  7.2 31.4 %corona_helio.1 = (f32[8,16,16,128]{3,2,1,0:T(8,128)S(1)}, f32[8,32,128]{2,1,0:T(8,128)S(1)}) custom-call(f32[8,16,16,128]{3,2,1,0:T(8,128)S(1)} %copy-done, f32[16,16,128]{2,1,0:T(8,128)S(1)} %copy-done.1, f32[8,8]{1,0:T(8,128)S(1)} %copy-done.7, f32[8,32,128]{2,1,0:T(8,128)S(1)} %copy-done.2, s32[1,2048]{1,0:T(1,128)S(1)} %bitcast.3, ...), custom_call_target="tpu_custom_call" | custom-call | tf_op jit(solution)/shard_map/corona_helio/pallas_call | solution.py:404
  38.7 1.0 %copy.12 = f32[8,16,16,128]{3,2,1,0:T(8,128)} copy(f32[8,16,16,128]{3,2,1,0:T(8,128)S(1)} %get-tuple-element.4) | data formatting | bytes 2097152
  39.6 0.7 %copy.13 = f32[8,32,128]{2,1,0:T(8,128)} copy(f32[8,32,128]{2,1,0:T(8,128)S(1)} %get-tuple-element.5) | data formatting | bytes 262144
Async XLA Ops:
  0.6 0.7 %copy-start.7 = (f32[8,8]{1,0:T(8,128)S(1)}, f32[8,8]{1,0:T(8,128)}, u32[]{:S(2)}) copy-start(f32[8,8]{1,0:T(8,128)} %mix.1) | copy-start | bytes 772
  1.3 1.2 %copy-start = (f32[8,16,16,128]{3,2,1,0:T(8,128)S(1)}, f32[8,16,16,128]{3,2,1,0:T(8,128)}, u32[]{:S(2)}) copy-start(f32[8,16,16,128]{3,2,1,0:T(8,128)} %corona.1) | copy-start | bytes 3145732
  2.5 0.9 %copy-start.1 = (f32[16,16,128]{2,1,0:T(8,128)S(1)}, f32[16,16,128]{2,1,0:T(8,128)}, u32[]{:S(2)}) copy-start(f32[16,16,128]{2,1,0:T(8,128)} %kappa.1) | copy-start | bytes 393220
  3.5 0.9 %copy-start.2 = (f32[8,32,128]{2,1,0:T(8,128)S(1)}, f32[8,32,128]{2,1,0:T(8,128)}, u32[]{:S(2)}) copy-start(f32[8,32,128]{2,1,0:T(8,128)} %helio.1) | copy-start | bytes 393220
  4.4 0.8 %copy-start.3 = (f32[3,2048]{1,0:T(4,128)S(1)}, f32[3,2048]{1,0:T(4,128)}, u32[]{:S(2)}) copy-start(f32[3,2048]{1,0:T(4,128)} %frac.1) | copy-start | bytes 73732
  5.1 0.7 %copy-start.4 = (s32[2048,1]{0,1:T(1,128)S(1)}, s32[2048,1]{0,1:T(1,128)}, u32[]{:S(2)}) copy-start(s32[2048,1]{0,1:T(1,128)} %param.12) | copy-start | bytes 24580
  5.8 0.7 %copy-start.5 = (s32[2048]{0:T(1024)S(1)}, s32[2048]{0:T(1024)}, u32[]{:S(2)}) copy-start(s32[2048]{0:T(1024)} %param.13) | copy-start | bytes 24580
  6.5 0.7 %copy-start.6 = (s32[2048]{0:T(1024)S(1)}, s32[2048]{0:T(1024)}, u32[]{:S(2)}) copy-start(s32[2048]{0:T(1024)} %param.14) | copy-start | bytes 24580

commit v2 on v1

--- a/solution.py
+++ b/solution.py
@@ -61,9 +61,9 @@
 
 
 def kernel(
-    n_lat, n_lon, corona, kappa, mix, helio, owner, dest, base, frac, stepped, face,
-    ue, sp, pleft, pright, q2, cs, cr, first, fleft, fright, st, pk, ds, rd, vs, rv,
-    shell, hs, hr, ts, tr, acc, load_sem, halo_send, halo_recv, out_sem,
+    n_lat, n_lon, corona, kappa, mix_in, helio_in, owner_in, dest_in, base_in, frac_in, stepped, face_out,
+    mix, helio, owner, dest, base, frac, face, ue, sp, pleft, pright, q2, cs, cr, first, fleft, fright, st, pk, ds, rd, vs, rv,
+    shell, hs, hr, ts, tr, acc, load_sem, halo_send, halo_recv, out_sem, face_sem,
     dest_send, dest_recv, val_send, val_recv, face_send, face_recv,
 ):
     n_dev = n_lat * n_lon
@@ -76,6 +76,11 @@
     loads = [
         pltpu.make_async_copy(corona, ue.at[0:fields, 2 : 2 + tt], load_sem.at[0]),
         pltpu.make_async_copy(kappa, ue.at[fields, 2 : 2 + tt], load_sem.at[1]),
+    ] + [
+        pltpu.make_async_copy(src, dst, load_sem.at[2 + k])
+        for k, (src, dst) in enumerate(
+            ((owner_in, owner), (base_in, base), (frac_in, frac), (dest_in, dest), (mix_in, mix), (helio_in, helio))
+        )
     ]
     for copy in loads:
         copy.start()
@@ -90,7 +95,7 @@
         return carry
 
     lax.fori_loop(1, n_dev, greet, 0)
-    for copy in loads:
+    for copy in loads[:2]:
         copy.wait()
 
     for j, p in enumerate((0, 1, pp - 2, pp - 1)):
@@ -138,6 +143,9 @@
         @pl.when(jnp.logical_not(inside(-a, -b)))
         def _(dst=dst):
             dst[...] = jnp.zeros(dst.shape, F32)
+
+    for copy in loads[2:]:
+        copy.wait()
 
     own = owner[...]
     upper = (iota((LANES, LANES), 0) < iota((LANES, LANES), 1)).astype(F32).astype(BF16)
@@ -372,6 +380,8 @@
         precision=lax.Precision.HIGHEST, preferred_element_type=F32,
     ).reshape(coupled.shape)
     face[...] = coupled + 0.2 * (inner + (down + up) + sides)
+    write_face = pltpu.make_async_copy(face, face_out, face_sem)
+    write_face.start()
 
     for k, ((a, b), src, dst) in enumerate(moves):
 
@@ -388,6 +398,7 @@
     all_dest.wait_send()
     all_vals.wait_send()
     write.wait()
+    write_face.wait()
 
 
 def body(corona, kappa, mixing, helio_prev, owner, dest_cell, corner_base, fractions):
@@ -397,7 +408,6 @@
     count = corner_base.shape[0]
     face_p, face_t = helio_prev.shape[1:]
     ext = fields + 1
-    vmem = pl.BlockSpec(memory_space=pltpu.VMEM)
     hbm = pl.BlockSpec(memory_space=pl.ANY)
     sem = pltpu.SemaphoreType.DMA
     v = lambda *shape: pltpu.VMEM(shape, F32)
@@ -407,9 +417,16 @@
             jax.ShapeDtypeStruct(corona.shape, F32),
             jax.ShapeDtypeStruct(helio_prev.shape, F32),
         ),
-        in_specs=[hbm, hbm, pl.BlockSpec(memory_space=pltpu.SMEM)] + [vmem] * 5,
-        out_specs=(hbm, vmem),
+        in_specs=[hbm] * 8,
+        out_specs=(hbm, hbm),
         scratch_shapes=[
+            pltpu.SMEM(mixing.shape, F32),
+            v(*helio_prev.shape),
+            pltpu.VMEM((1, count), jnp.int32),
+            pltpu.VMEM((1, count), jnp.int32),
+            pltpu.VMEM((1, count), jnp.int32),
+            v(3, count),
+            v(*helio_prev.shape),
             v(ext, tt + 4, pp, n_r),
             v(4, ext, tt, n_r),
             v(ext, tt + 16, n_r),
@@ -432,11 +449,11 @@
             v(8, fields * face_p),
             v(2, 8, fields * face_p),
             v(2 * fields * face_p, face_t),
-            sem((2,)), sem((10,)), sem((10,)), sem,
+            sem((8,)), sem((10,)), sem((10,)), sem, sem,
             sem, sem, sem, sem, sem((4,)), sem((4,)),
         ],
         compiler_params=pltpu.CompilerParams(
-            collective_id=0, has_side_effects=True, vmem_limit_bytes=48 * 1024 * 1024
+            collective_id=0, has_side_effects=True, vmem_limit_bytes=63 * 1024 * 1024
         ),
         name="corona_helio",
     )(

time: 40.7 us -> 35 us (0.86)
  local copies, waits for them, and re-layouts: 8.19 us -> 2.96 us
    unnamed x18 -> x4, local copies, waits for them, and re-layouts: 8.19 us -> 2.96 us
where the time goes in v2:
time: 35 us; the launch traced here: 34.9 us
  Pallas kernels  31.3 us (89%)
  local copies, waits for them, and re-layouts  2.96 us (8%)
  between operations  0.65 us (2%)
    pallas_call x1, Pallas kernels, body(): pl.pallas_call(functools.partial(kernel, n_lat, n_lon), out_shape=(jax.Sh...  31.3 us
    unnamed x4, local copies, waits for them, and re-layouts  2.96 us

profile of v2, /device:TPU:0, one launch (start us, length us, event | category | flops | bytes accessed | tf_op | source)
XLA Modules:
  0.0 34.9 jit_solution(9196698624914015067)
XLA Ops:
  0.6 31.3 %corona_helio.1 = (f32[8,16,16,128]{3,2,1,0:T(8,128)}, f32[8,32,128]{2,1,0:T(8,128)}) custom-call(f32[8,16,16,128]{3,2,1,0:T(8,128)} %corona.1, f32[16,16,128]{2,1,0:T(8,128)} %kappa.1, f32[8,8]{1,0:T(8,128)} %mix_in.1, f32[8,32,128]{2,1,0:T(8,128)} %helio_in.1, s32[1,2048]{1,0:T(1,128)} %bitcast.3, s32[1,2048]{1,0:T(1,128)} %bitcast.4, s32[1,2048]{1,0:T(1,128)} %bitcast.5, ...), custom_call_target="tpu_custom_call" | custom-call | tf_op jit(solution)/shard_map/corona_helio/pallas_call | solution.py:414
  31.9 0.0 copy-start
  31.9 2.3 %copy.12 = f32[8,16,16,128]{3,2,1,0:T(8,128)} copy(f32[8,16,16,128]{3,2,1,0:T(8,128)} %get-tuple-element.4) | data formatting | bytes 2097152
  34.2 0.0 copy-done
  34.2 0.7 %copy.13 = f32[8,32,128]{2,1,0:T(8,128)} copy(f32[8,32,128]{2,1,0:T(8,128)S(1)} %copy-done) | data formatting | bytes 262144
Async XLA Ops:
  31.9 2.3 %copy-start = (f32[8,32,128]{2,1,0:T(8,128)S(1)}, f32[8,32,128]{2,1,0:T(8,128)}, u32[]{:S(2)}) copy-start(f32[8,32,128]{2,1,0:T(8,128)} %get-tuple-element.5) | copy-start | bytes 393220

commit v3 on v2

--- a/solution.py
+++ b/solution.py
@@ -15,6 +15,8 @@
 GROUP = 8
 LAND = 4
 NPAR = 5
+DEEP = 16
+WIDE = 4 * LANES
 
 
 def iota(shape, dim):
@@ -62,8 +64,8 @@
 
 def kernel(
     n_lat, n_lon, corona, kappa, mix_in, helio_in, owner_in, dest_in, base_in, frac_in, stepped, face_out,
-    mix, helio, owner, dest, base, frac, face, ue, sp, pleft, pright, q2, cs, cr, first, fleft, fright, st, pk, ds, rd, vs, rv,
-    shell, hs, hr, ts, tr, acc, load_sem, halo_send, halo_recv, out_sem, face_sem,
+    mix, mixv, helio, owner, dest, base, frac, face, xe, ke, xm, xf, co, ue, sp, pleft, pright, q2, cs, cr, first, fleft, fright, st, pk, ds, rd, vs, rv,
+    shell, hs, hr, ts, tr, acc, load_sem, halo_send, halo_recv, small_send, small_recv, out_sem, face_sem,
     dest_send, dest_recv, val_send, val_recv, face_send, face_recv,
 ):
     n_dev = n_lat * n_lon
@@ -79,7 +81,7 @@
     ] + [
         pltpu.make_async_copy(src, dst, load_sem.at[2 + k])
         for k, (src, dst) in enumerate(
-            ((owner_in, owner), (base_in, base), (frac_in, frac), (dest_in, dest), (mix_in, mix), (helio_in, helio))
+            ((owner_in, owner), (base_in, base), (frac_in, frac), (dest_in, dest), (mix_in, mix), (mix_in, mixv), (helio_in, helio))
         )
     ]
     for copy in loads:
@@ -98,14 +100,33 @@
     for copy in loads[:2]:
         copy.wait()
 
-    for j, p in enumerate((0, 1, pp - 2, pp - 1)):
-        sp[j] = ue[:, 2 : 2 + tt, p, :]
+    per = LANES // DEEP
+    lane1 = iota((1, LANES), 1)
+
+    def extract(t, carry):
+        lane = iota((fields, LANES), 1) // DEEP
+        for h in range(pp // per):
+            row = jnp.zeros((fields, LANES), F32)
+            for j in range(per):
+                x = pltpu.roll(ue[0:fields, t + 2, h * per + j, :], (j + 1) * DEEP % LANES, 1)
+                row = jnp.where(lane == j, x, row)
+            xe[t + 2, :, (h + 1) * LANES : (h + 2) * LANES] = row
+        return carry
+
+    lax.fori_loop(0, tt, extract, 0)
+    lane_t = iota((tt, LANES), 1) // DEEP
+    for h in range(pp // per):
+        row = jnp.zeros((tt, LANES), F32)
+        for j in range(per):
+            x = pltpu.roll(ue[fields, 2 : 2 + tt, h * per + j, :], (j + 1) * DEEP % LANES, 1)
+            row = jnp.where(lane_t == j, x, row)
+        ke[2 : 2 + tt, :, (h + 1) * LANES : (h + 2) * LANES] = row[:, None, :]
+    for ref in (xe, ke):
+        for t in (0, tt + 3):
+            for lo in (0, WIDE - LANES):
+                ref[t, :, lo : lo + LANES] = jnp.zeros((ref.shape[1], LANES), F32)
+
     corners = [(1, 1), (1, -1), (-1, 1), (-1, -1)]
-    for k, (a, b) in enumerate(corners):
-        t, p = (2 + tt - 1 if a > 0 else 2), (pp - 1 if b > 0 else 0)
-        for f in range(fields + 1):
-            cs[k, f : f + 1, :] = ue[f, t, p : p + 1, :]
-
     moves = [
         ((1, 0), ue.at[:, tt : tt + 2], ue.at[:, 0:2]),
         ((-1, 0), ue.at[:, 2:4], ue.at[:, tt + 2 : tt + 4]),
@@ -114,6 +135,26 @@
         ((0, -1), sp.at[0], pright.at[:, 8 : 8 + tt]),
         ((0, -1), sp.at[1], q2.at[1]),
     ] + [(ab, cs.at[k], cr.at[k]) for k, ab in enumerate(corners)]
+
+    mid = slice(LANES, WIDE - LANES)
+    rows_in = slice(2, 2 + tt)
+    places = [
+        ((1, 0), (slice(tt, tt + 2), mid), (slice(0, 2), mid)),
+        ((-1, 0), (slice(2, 4), mid), (slice(tt + 2, tt + 4), mid)),
+        ((0, 1), (rows_in, slice(2 * LANES, 3 * LANES)), (rows_in, slice(0, LANES))),
+        ((0, -1), (rows_in, slice(LANES, 2 * LANES)), (rows_in, slice(3 * LANES, WIDE))),
+    ]
+    for a, b in corners:
+        src_t = slice(tt + 1, tt + 2) if a > 0 else slice(2, 3)
+        dst_t = slice(1, 2) if a > 0 else slice(tt + 2, tt + 3)
+        src_l = slice(2 * LANES, 3 * LANES) if b > 0 else slice(LANES, 2 * LANES)
+        dst_l = slice(0, LANES) if b > 0 else slice(3 * LANES, WIDE)
+        places.append(((a, b), (src_t, src_l), (dst_t, dst_l)))
+    small = [
+        (ab, ref.at[src[0], :, src[1]], ref.at[dst[0], :, dst[1]])
+        for ab, src, dst in places
+        for ref in (xe, ke)
+    ]
 
     def inside(a, b):
         ok = lat >= 0
@@ -133,16 +174,41 @@
             device_id=(lat + a, lon + b), device_id_type=MESH,
         )
 
+    def launch(todo, send, recv):
+        for k, ((a, b), src, dst) in enumerate(todo):
+
+            @pl.when(inside(a, b))
+            def _(k=k, a=a, b=b, src=src, dst=dst):
+                remote(a, b, src, dst, send.at[k], recv.at[k]).start()
+
+            @pl.when(jnp.logical_not(inside(-a, -b)))
+            def _(dst=dst):
+                dst[...] = jnp.zeros(dst.shape, F32)
+
+    def arrive(todo, send, recv):
+        for k, ((a, b), src, dst) in enumerate(todo):
+
+            @pl.when(inside(-a, -b))
+            def _(k=k, a=a, b=b, src=src, dst=dst):
+                remote(-a, -b, src, dst, send.at[k], recv.at[k]).wait_recv()
+
+    def leave(todo, send, recv):
+        for k, ((a, b), src, dst) in enumerate(todo):
+
+            @pl.when(inside(a, b))
+            def _(k=k, a=a, b=b, src=src, dst=dst):
+                remote(a, b, src, dst, send.at[k], recv.at[k]).wait_send()
+
     pl.semaphore_wait(barrier, n_dev - 1)
-    for k, ((a, b), src, dst) in enumerate(moves):
-
-        @pl.when(inside(a, b))
-        def _(k=k, a=a, b=b, src=src, dst=dst):
-            remote(a, b, src, dst, halo_send.at[k], halo_recv.at[k]).start()
-
-        @pl.when(jnp.logical_not(inside(-a, -b)))
-        def _(dst=dst):
-            dst[...] = jnp.zeros(dst.shape, F32)
+    launch(small, small_send, small_recv)
+    for j, p in enumerate((0, 1, pp - 2, pp - 1)):
+        sp[j] = ue[:, 2 : 2 + tt, p, :]
+    for k, (a, b) in enumerate(corners):
+        t, p = (2 + tt - 1 if a > 0 else 2), (pp - 1 if b > 0 else 0)
+        for f in range(fields + 1):
+            cs[k, f : f + 1, :] = ue[f, t, p : p + 1, :]
+
+    launch(moves, halo_send, halo_recv)
 
     for copy in loads[2:]:
         copy.wait()
@@ -197,12 +263,109 @@
     lax.fori_loop(1, n_dev, send_dest, 0)
     rd[me] = ds[me]
 
-    for k, ((a, b), src, dst) in enumerate(moves):
-
-        @pl.when(inside(-a, -b))
-        def _(k=k, a=a, b=b, src=src, dst=dst):
-            remote(-a, -b, src, dst, halo_send.at[k], halo_recv.at[k]).wait_recv()
-
+    nrow = (tt + 2) * fields
+    hot = jnp.where(iota((nrow, fields), 0) % fields == iota((nrow, fields), 1), 1.0, 0.0)
+    wide_mix = lax.dot_general(
+        jnp.dot(hot, 0.3 * mixv[...], precision=lax.Precision.HIGHEST, preferred_element_type=F32),
+        hot, (((1,), (1,)), ((), ())), precision=lax.Precision.HIGHEST, preferred_element_type=F32,
+    )
+    same = iota((nrow, nrow), 0) // fields == iota((nrow, nrow), 1) // fields
+    m_hi, m_lo = split(jnp.where(same, wide_mix, 0.0))
+
+    def mixed(x, n):
+        hi, lo = split(x)
+        mh, ml = m_hi[:n, :n], m_lo[:n, :n]
+        dot = lambda a, b: jnp.dot(a, b, preferred_element_type=F32)
+        return dot(mh, hi) + (dot(mh, lo) + dot(ml, hi))
+
+    arrive(small, small_send, small_recv)
+    xm[...] = mixed(xe[1 : tt + 3].reshape(nrow, WIDE), nrow).reshape(tt + 2, fields, WIDE)
+    lane = iota((1, WIDE), 1)
+    top = lane % DEEP == DEEP - 1
+    outside = ((lane < LANES) & (lon == 0)) | ((lane >= WIDE - LANES) & (lon == n_lon - 1))
+    keep_lane = jnp.where(outside, 0.0, 1.0)
+
+    def roll(x, by):
+        return pltpu.roll(x, by % WIDE, 1)
+
+    def compact_row(c, up, down, k, more):
+        return (
+            more + k[6] * c + (k[0] * up + k[1] * down) + (k[2] * roll(c, DEEP) + k[3] * roll(c, -DEEP))
+            + (k[4] * roll(c, 1) + k[5] * roll(c, -1))
+        )
+
+    def compact_first(i, carry):
+        kc = ke[i + 1]
+        k = [0.075 * (kc + x) for x in (ke[i], ke[i + 2], roll(kc, DEEP), roll(kc, -DEEP), roll(kc, 1))]
+        outer = 0.075 * (kc + jnp.where(top, 0.0, roll(kc, -1)))
+        diag = 1.0 - (((k[0] + k[1]) + (k[2] + k[3])) + (k[4] + outer))
+        k += [jnp.where(top, 0.0, outer), diag]
+        off = ((i == 0) & (lat == 0)) | ((i == tt + 1) & (lat == n_lat - 1))
+        keep = keep_lane * jnp.where(off, 0.0, 1.0)
+        xf[i] = keep * compact_row(xe[i + 1], xe[i], xe[i + 2], k, xm[i])
+
+        @pl.when((i > 0) & (i < tt + 1))
+        def _():
+            for q in range(7):
+                co[i - 1, q] = k[q]
+
+        return carry
+
+    lax.fori_loop(0, tt + 2, compact_first, 0)
+    xm[0:tt] = mixed(xf[1 : tt + 1].reshape(tt * fields, WIDE), tt * fields).reshape(tt, fields, WIDE)
+
+    def compact_second(t, carry):
+        out = compact_row(xf[t + 1], xf[t], xf[t + 2], [co[t, q] for q in range(7)], xm[t])
+        shell[t] = out[:, mid]
+        return carry
+
+    lax.fori_loop(0, tt, compact_second, 0)
+    deep_at, cell_at = iota((2 * LANES, LANES), 0), iota((2 * LANES, LANES), 1)
+    take = jnp.where(
+        (deep_at // DEEP == cell_at // SH) & (deep_at % DEEP == cell_at % SH + DEEP - SH), 1.0, 0.0
+    ).astype(BF16)
+    s_hi, s_lo = [
+        jnp.dot(x, take, preferred_element_type=F32).astype(BF16)
+        for x in split(shell[...].reshape(tt * fields, 2 * LANES))
+    ]
+    left = jnp.concatenate([s_hi, s_hi, s_lo], axis=1)
+    groups = n_dev // GROUP
+    wide = GROUP * LANES
+
+    def values(i, carry):
+        g = lax.rem(lax.div(me, GROUP) + i, groups)
+        par = [
+            jnp.concatenate([pk[g, q, k : k + 1, :] for k in range(GROUP)], axis=1)
+            for q in range(NPAR - 1)
+        ]
+        cell = par[0].astype(jnp.int32)
+        t0, p0, r0 = cell >> 7, (cell >> 3) & 15, cell & 7
+        fx, fy, fz = par[1:]
+
+        def weights(n, at, fr):
+            idx = iota((n, wide), 0) - at
+            return jnp.where(idx == 0, 1.0 - fr, jnp.where(idx == 1, fr, 0.0))
+
+        wa, wb, wc = weights(tt, t0, fx), weights(pp, p0, fy), weights(SH, r0, fz)
+        table = (wb[:, None, :] * wc[None]).reshape(pp * SH, wide)
+        hi, lo = split(table)
+        got = jnp.dot(left, jnp.concatenate([hi, lo, hi], axis=0), preferred_element_type=F32)
+        val = jnp.sum(got.reshape(tt, fields, wide) * wa[:, None, :], axis=0)
+        for k in range(GROUP):
+            vs[g * GROUP + k] = val[:, k * LANES : (k + 1) * LANES]
+        for k in range(GROUP):
+            o = g * GROUP + k
+
+            @pl.when(o != me)
+            def _(o=o):
+                send_to(o, vs.at[o], rv.at[me], val_send, val_recv).start()
+
+        return carry
+
+    lax.fori_loop(0, groups, values, 0)
+    rv[me] = vs[me]
+
+    arrive(moves, halo_send, halo_recv)
     for k, (a, b) in enumerate(corners):
         side = pleft if b > 0 else pright
         row = 7 if a > 0 else 8 + tt
@@ -234,75 +397,6 @@
         keep = jnp.where(ok, 1.0, 0.0)
         for g in range(fields):
             into[g] = out[g] * keep
-
-    def second_row(t, carry):
-        c = first[:, t + 1]
-        low, high = shift_rows(c, fleft[:, pl.ds(t, 1), :], fright[:, pl.ds(t, 1), :])
-        kc = ue[fields:, t + 2]
-        klow, khigh = shift_rows(
-            kc, pleft[fields:, pl.ds(8 + t, 1), :], pright[fields:, pl.ds(8 + t, 1), :]
-        )
-        out = apply_step(
-            c, [first[:, t], first[:, t + 2], low, high],
-            kc[0], [ue[fields, t + 1], ue[fields, t + 3], klow[0], khigh[0]], mix,
-        )
-        for g in range(fields):
-            st[g, t] = out[g]
-        return carry
-
-    lax.fori_loop(0, tt, second_row, 0)
-    write = pltpu.make_async_copy(st, stepped, out_sem)
-    write.start()
-
-    n_r = st.shape[3]
-
-    def shell_row(t, carry):
-        lane = iota((fields, LANES), 1)
-        row = jnp.zeros((fields, LANES), F32)
-        for p in range(pp):
-            x = pltpu.roll(st[:, t, p, :], (p * SH + SH) % n_r, 1)
-            row = jnp.where((lane >= p * SH) & (lane < (p + 1) * SH), x, row)
-        shell[t] = row
-        return carry
-
-    lax.fori_loop(0, tt, shell_row, 0)
-    s_hi, s_lo = split(shell[...].reshape(tt * fields, LANES))
-    left = jnp.concatenate([s_hi, s_hi, s_lo], axis=1)
-    groups = n_dev // GROUP
-    wide = GROUP * LANES
-
-    def values(i, carry):
-        g = lax.rem(lax.div(me, GROUP) + i, groups)
-        par = [
-            jnp.concatenate([pk[g, q, k : k + 1, :] for k in range(GROUP)], axis=1)
-            for q in range(NPAR - 1)
-        ]
-        cell = par[0].astype(jnp.int32)
-        t0, p0, r0 = cell >> 7, (cell >> 3) & 15, cell & 7
-        fx, fy, fz = par[1:]
-
-        def weights(n, at, fr):
-            idx = iota((n, wide), 0) - at
-            return jnp.where(idx == 0, 1.0 - fr, jnp.where(idx == 1, fr, 0.0))
-
-        wa, wb, wc = weights(tt, t0, fx), weights(pp, p0, fy), weights(SH, r0, fz)
-        table = (wb[:, None, :] * wc[None]).reshape(pp * SH, wide)
-        hi, lo = split(table)
-        got = jnp.dot(left, jnp.concatenate([hi, lo, hi], axis=0), preferred_element_type=F32)
-        val = jnp.sum(got.reshape(tt, fields, wide) * wa[:, None, :], axis=0)
-        for k in range(GROUP):
-            vs[g * GROUP + k] = val[:, k * LANES : (k + 1) * LANES]
-        for k in range(GROUP):
-            o = g * GROUP + k
-
-            @pl.when(o != me)
-            def _(o=o):
-                send_to(o, vs.at[o], rv.at[me], val_send, val_recv).start()
-
-        return carry
-
-    lax.fori_loop(0, groups, values, 0)
-    rv[me] = vs[me]
 
     other = lax.rem(me + 1, n_dev)
     all_dest = send_to(other, ds.at[0 : n_dev - 1], rd.at[0 : n_dev - 1], dest_send, dest_recv)
@@ -347,15 +441,29 @@
         ((1, 0), ts, tr.at[0]),
         ((-1, 0), ts, tr.at[1]),
     ]
-    for k, ((a, b), src, dst) in enumerate(edges):
-
-        @pl.when(inside(a, b))
-        def _(k=k, a=a, b=b, src=src, dst=dst):
-            remote(a, b, src, dst, face_send.at[k], face_recv.at[k]).start()
-
-        @pl.when(jnp.logical_not(inside(-a, -b)))
-        def _(dst=dst):
-            dst[...] = jnp.zeros(dst.shape, F32)
+    launch(edges, face_send, face_recv)
+
+    def second_row(t, carry):
+        c = first[:, t + 1]
+        low, high = shift_rows(c, fleft[:, pl.ds(t, 1), :], fright[:, pl.ds(t, 1), :])
+        kc = ue[fields:, t + 2]
+        klow, khigh = shift_rows(
+            kc, pleft[fields:, pl.ds(8 + t, 1), :], pright[fields:, pl.ds(8 + t, 1), :]
+        )
+        out = apply_step(
+            c, [first[:, t], first[:, t + 2], low, high],
+            kc[0], [ue[fields, t + 1], ue[fields, t + 3], klow[0], khigh[0]], mix,
+        )
+        for g in range(fields):
+            st[g, t] = out[g]
+        return carry
+
+    writes = []
+    for h in range(2):
+        part = slice(h * (tt // 2), (h + 1) * (tt // 2))
+        lax.fori_loop(part.start, part.stop, second_row, 0)
+        writes.append(pltpu.make_async_copy(st.at[:, part], stepped.at[:, part], out_sem.at[h]))
+        writes[h].start()
 
     lane3 = iota(coupled.shape, 2)
     inner = (
@@ -363,12 +471,7 @@
         + jnp.where(lane3 == face_t - 1, 0.0, pltpu.roll(coupled, face_t - 1, 2))
         - 4.0 * coupled
     )
-    for k, ((a, b), src, dst) in enumerate(edges):
-
-        @pl.when(inside(-a, -b))
-        def _(k=k, a=a, b=b, src=src, dst=dst):
-            remote(-a, -b, src, dst, face_send.at[k], face_recv.at[k]).wait_recv()
-
+    arrive(edges, face_send, face_recv)
     lows = jnp.concatenate([hr[0, f : f + 1, :][None] for f in range(fields)], axis=0)
     highs = jnp.concatenate([hr[1, f : f + 1, :][None] for f in range(fields)], axis=0)
     down, up = shift_rows(coupled, lows, highs)
@@ -383,21 +486,13 @@
     write_face = pltpu.make_async_copy(face, face_out, face_sem)
     write_face.start()
 
-    for k, ((a, b), src, dst) in enumerate(moves):
-
-        @pl.when(inside(a, b))
-        def _(k=k, a=a, b=b, src=src, dst=dst):
-            remote(a, b, src, dst, halo_send.at[k], halo_recv.at[k]).wait_send()
-
-    for k, ((a, b), src, dst) in enumerate(edges):
-
-        @pl.when(inside(a, b))
-        def _(k=k, a=a, b=b, src=src, dst=dst):
-            remote(a, b, src, dst, face_send.at[k], face_recv.at[k]).wait_send()
-
+    leave(small, small_send, small_recv)
+    leave(moves, halo_send, halo_recv)
+    leave(edges, face_send, face_recv)
     all_dest.wait_send()
     all_vals.wait_send()
-    write.wait()
+    for copy in writes:
+        copy.wait()
     write_face.wait()
 
 
@@ -408,7 +503,8 @@
     count = corner_base.shape[0]
     face_p, face_t = helio_prev.shape[1:]
     ext = fields + 1
-    hbm = pl.BlockSpec(memory_space=pl.ANY)
+    hbm = pl.BlockSpec(memory_space=pltpu.HBM)
+    free = pl.BlockSpec(memory_space=pl.ANY)
     sem = pltpu.SemaphoreType.DMA
     v = lambda *shape: pltpu.VMEM(shape, F32)
     return pl.pallas_call(
@@ -418,15 +514,21 @@
             jax.ShapeDtypeStruct(helio_prev.shape, F32),
         ),
         in_specs=[hbm] * 8,
-        out_specs=(hbm, hbm),
+        out_specs=(free, free),
         scratch_shapes=[
             pltpu.SMEM(mixing.shape, F32),
+            v(*mixing.shape),
             v(*helio_prev.shape),
             pltpu.VMEM((1, count), jnp.int32),
             pltpu.VMEM((1, count), jnp.int32),
             pltpu.VMEM((1, count), jnp.int32),
             v(3, count),
             v(*helio_prev.shape),
+            v(tt + 4, fields, WIDE),
+            v(tt + 4, 1, WIDE),
+            v(tt + 2, fields, WIDE),
+            v(tt + 2, fields, WIDE),
+            v(tt, 7, 1, WIDE),
             v(ext, tt + 4, pp, n_r),
             v(4, ext, tt, n_r),
             v(ext, tt + 16, n_r),
@@ -443,13 +545,13 @@
             v(n_dev, 1, LANES),
             v(n_dev, fields, LANES),
             v(n_dev, fields, LANES),
-            v(tt, fields, LANES),
+            v(tt, fields, 2 * LANES),
             v(2, fields, face_t),
             v(2, fields, face_t),
             v(8, fields * face_p),
             v(2, 8, fields * face_p),
             v(2 * fields * face_p, face_t),
-            sem((8,)), sem((10,)), sem((10,)), sem, sem,
+            sem((9,)), sem((10,)), sem((10,)), sem((16,)), sem((16,)), sem((2,)), sem,
             sem, sem, sem, sem, sem((4,)), sem((4,)),
         ],
         compiler_params=pltpu.CompilerParams(

time: 35 us -> 31.2 us (0.89)
  Pallas kernels: 31.3 us -> 27.4 us
    pallas_call x1, Pallas kernels: 31.3 us -> 27.4 us  [body(): pl.pallas_call(functools.partial(kernel, n_lat, n_lon), out_shape=(jax.Sh...]
where the time goes in v3:
time: 31.2 us; the launch traced here: 31.1 us
  Pallas kernels  27.4 us (88%)
  local copies, waits for them, and re-layouts  2.96 us (9%)
  between operations  0.65 us (2%)
    pallas_call x1, Pallas kernels, body(): pl.pallas_call(functools.partial(kernel, n_lat, n_lon), out_shape=(jax.Sh...  27.4 us
    unnamed x4, local copies, waits for them, and re-layouts  2.96 us

profile of v3, /device:TPU:0, one launch (start us, length us, event | category | flops | bytes accessed | tf_op | source)
XLA Modules:
  0.0 31.1 jit_solution(11531676134396200238)
XLA Ops:
  0.6 27.4 %corona_helio.1 = (f32[8,16,16,128]{3,2,1,0:T(8,128)}, f32[8,32,128]{2,1,0:T(8,128)}) custom-call(f32[8,16,16,128]{3,2,1,0:T(8,128)} %corona.1, f32[16,16,128]{2,1,0:T(8,128)} %kappa.1, f32[8,8]{1,0:T(8,128)} %mix_in.1, f32[8,32,128]{2,1,0:T(8,128)} %helio_in.1, s32[1,2048]{1,0:T(1,128)} %bitcast.3, s32[1,2048]{1,0:T(1,128)} %bitcast.4, s32[1,2048]{1,0:T(1,128)} %bitcast.5, ...), custom_call_target="tpu_custom_call" | custom-call | tf_op jit(solution)/shard_map/corona_helio/pallas_call | solution.py:510
  28.1 0.0 copy-start
  28.1 2.3 %copy.12 = f32[8,16,16,128]{3,2,1,0:T(8,128)} copy(f32[8,16,16,128]{3,2,1,0:T(8,128)} %get-tuple-element.4) | data formatting | bytes 2097152
  30.4 0.0 copy-done
  30.4 0.7 %copy.13 = f32[8,32,128]{2,1,0:T(8,128)} copy(f32[8,32,128]{2,1,0:T(8,128)S(1)} %copy-done) | data formatting | bytes 262144
Async XLA Ops:
  28.1 2.3 %copy-start = (f32[8,32,128]{2,1,0:T(8,128)S(1)}, f32[8,32,128]{2,1,0:T(8,128)}, u32[]{:S(2)}) copy-start(f32[8,32,128]{2,1,0:T(8,128)} %get-tuple-element.5) | copy-start | bytes 393220

commit v4 on v3

--- a/solution.py
+++ b/solution.py
@@ -555,12 +555,17 @@
             sem, sem, sem, sem, sem((4,)), sem((4,)),
         ],
         compiler_params=pltpu.CompilerParams(
-            collective_id=0, has_side_effects=True, vmem_limit_bytes=63 * 1024 * 1024
+            collective_id=0, has_side_effects=True, vmem_limit_bytes=48 * 1024 * 1024
         ),
         name="corona_helio",
     )(
-        corona, kappa, mixing, helio_prev, owner.reshape(1, count), dest_cell.reshape(1, count),
-        corner_base.reshape(1, count), fractions,
+        *[
+            pltpu.with_memory_space_constraint(x, pltpu.HBM)
+            for x in (
+                corona, kappa, mixing, helio_prev, owner.reshape(1, count), dest_cell.reshape(1, count),
+                corner_base.reshape(1, count), fractions,
+            )
+        ]
     )
 
 

time: 31.2 us -> 29.5 us (0.946)
  local copies, waits for them, and re-layouts: 2.96 us -> 1.63 us
  Pallas kernels: 27.4 us -> 27 us
    unnamed x4 -> x2, local copies, waits for them, and re-layouts: 2.96 us -> 1.63 us
    pallas_call x1, Pallas kernels: 27.4 us -> 27 us  [body(): pl.pallas_call(functools.partial(kernel, n_lat, n_lon), out_shape=(jax.Sh...]
where the time goes in v4:
time: 29.5 us; the launch traced here: 29.3 us
  Pallas kernels  27 us (92%)
  local copies, waits for them, and re-layouts  1.63 us (6%)
  between operations  0.64 us (2%)
    pallas_call x1, Pallas kernels, body(): pl.pallas_call(functools.partial(kernel, n_lat, n_lon), out_shape=(jax.Sh...  27 us
    unnamed x2, local copies, waits for them, and re-layouts  1.63 us

profile of v4, /device:TPU:0, one launch (start us, length us, event | category | flops | bytes accessed | tf_op | source)
XLA Modules:
  0.0 29.3 jit_solution(2792271339747238379)
XLA Ops:
  0.6 27.0 %corona_helio.1 = (f32[8,16,16,128]{3,2,1,0:T(8,128)S(1)}, f32[8,32,128]{2,1,0:T(8,128)S(1)}) custom-call(f32[8,16,16,128]{3,2,1,0:T(8,128)} %corona.1, f32[16,16,128]{2,1,0:T(8,128)} %kappa.1, f32[8,8]{1,0:T(8,128)} %mix_in.1, f32[8,32,128]{2,1,0:T(8,128)} %helio_in.1, s32[1,2048]{1,0:T(1,128)} %bitcast.3, s32[1,2048]{1,0:T(1,128)} %bitcast.4, ...), custom_call_target="tpu_custom_call" | custom-call | tf_op jit(solution)/shard_map/corona_helio/pallas_call | solution.py:510
  27.7 1.0 %copy.12 = f32[8,16,16,128]{3,2,1,0:T(8,128)} copy(f32[8,16,16,128]{3,2,1,0:T(8,128)S(1)} %get-tuple-element.4) | data formatting | bytes 2097152
  28.7 0.7 %copy.13 = f32[8,32,128]{2,1,0:T(8,128)} copy(f32[8,32,128]{2,1,0:T(8,128)S(1)} %get-tuple-element.5) | data formatting | bytes 262144

commit v5 on v4

--- a/solution.py
+++ b/solution.py
@@ -32,7 +32,7 @@
     return lax.dot_general(a, b, (((1,), (1,)), ((), ())), preferred_element_type=F32)
 
 
-def apply_step(c, near, kc, knear, mix):
+def apply_step(c, near, kc, knear, mb):
     lane = iota(kc.shape, 1)
     last = kc.shape[1] - 1
     ks = [0.075 * (kc + kn) for kn in knear]
@@ -45,13 +45,11 @@
     for k, u in zip(ks, near):
         total = total + k[None] * u
     total = total + kl[None] * pltpu.roll(c, 1, 2) + kr[None] * pltpu.roll(c, last, 2)
-    out = []
-    for g in range(c.shape[0]):
-        row = total[g]
-        for f in range(c.shape[0]):
-            row = row + (0.3 * mix[g, f]) * c[f]
-        out.append(row)
-    return out
+    tiles = (c.shape[1] // 8, 8, c.shape[2])
+    total = total.reshape((c.shape[0],) + tiles)
+    for f in range(c.shape[0]):
+        total = total + mb[f][:, None] * c[f].reshape(tiles)[None]
+    return total.reshape(c.shape)
 
 
 def shift_rows(c, low, high):
@@ -64,7 +62,7 @@
 
 def kernel(
     n_lat, n_lon, corona, kappa, mix_in, helio_in, owner_in, dest_in, base_in, frac_in, stepped, face_out,
-    mix, mixv, helio, owner, dest, base, frac, face, xe, ke, xm, xf, co, ue, sp, pleft, pright, q2, cs, cr, first, fleft, fright, st, pk, ds, rd, vs, rv,
+    mix, mixv, mb, helio, owner, dest, base, frac, face, xe, ke, xm, xf, co, ue, sp, pleft, pright, q2, cs, cr, first, fleft, fright, st, pk, ds, rd, vs, rv,
     shell, hs, hr, ts, tr, acc, load_sem, halo_send, halo_recv, small_send, small_recv, out_sem, face_sem,
     dest_send, dest_recv, val_send, val_recv, face_send, face_recv,
 ):
@@ -103,17 +101,18 @@
     per = LANES // DEEP
     lane1 = iota((1, LANES), 1)
 
-    def extract(t, carry):
+    def extract(i, carry):
         lane = iota((fields, LANES), 1) // DEEP
-        for h in range(pp // per):
-            row = jnp.zeros((fields, LANES), F32)
-            for j in range(per):
-                x = pltpu.roll(ue[0:fields, t + 2, h * per + j, :], (j + 1) * DEEP % LANES, 1)
-                row = jnp.where(lane == j, x, row)
-            xe[t + 2, :, (h + 1) * LANES : (h + 2) * LANES] = row
-        return carry
-
-    lax.fori_loop(0, tt, extract, 0)
+        for t in [4 * i + k for k in range(4)]:
+            for h in range(pp // per):
+                row = jnp.zeros((fields, LANES), F32)
+                for j in range(per):
+                    x = pltpu.roll(ue[0:fields, t + 2, h * per + j, :], (j + 1) * DEEP % LANES, 1)
+                    row = jnp.where(lane == j, x, row)
+                xe[t + 2, :, (h + 1) * LANES : (h + 2) * LANES] = row
+        return carry
+
+    lax.fori_loop(0, tt // 4, extract, 0)
     lane_t = iota((tt, LANES), 1) // DEEP
     for h in range(pp // per):
         row = jnp.zeros((tt, LANES), F32)
@@ -213,6 +212,10 @@
     for copy in loads[2:]:
         copy.wait()
 
+    for f in range(fields):
+        for g in range(fields):
+            mb[f, g] = jnp.full((8, LANES), 0.3 * mix[g, f], F32)
+
     own = owner[...]
     upper = (iota((LANES, LANES), 0) < iota((LANES, LANES), 1)).astype(F32).astype(BF16)
     carry = jnp.zeros((n_dev, 1), F32)
@@ -280,46 +283,50 @@
 
     arrive(small, small_send, small_recv)
     xm[...] = mixed(xe[1 : tt + 3].reshape(nrow, WIDE), nrow).reshape(tt + 2, fields, WIDE)
-    lane = iota((1, WIDE), 1)
+    lane = iota((1, 1, WIDE), 2)
     top = lane % DEEP == DEEP - 1
     outside = ((lane < LANES) & (lon == 0)) | ((lane >= WIDE - LANES) & (lon == n_lon - 1))
     keep_lane = jnp.where(outside, 0.0, 1.0)
 
     def roll(x, by):
-        return pltpu.roll(x, by % WIDE, 1)
-
-    def compact_row(c, up, down, k, more):
+        return pltpu.roll(x, by % WIDE, 2)
+
+    def compact_rows(c, up, down, k, more):
         return (
             more + k[6] * c + (k[0] * up + k[1] * down) + (k[2] * roll(c, DEEP) + k[3] * roll(c, -DEEP))
             + (k[4] * roll(c, 1) + k[5] * roll(c, -1))
         )
 
-    def compact_first(i, carry):
-        kc = ke[i + 1]
-        k = [0.075 * (kc + x) for x in (ke[i], ke[i + 2], roll(kc, DEEP), roll(kc, -DEEP), roll(kc, 1))]
+    def compact_first(j, carry):
+        n = 6
+        i = j * n
+        at = lambda ref, d: ref[pl.ds(i + d, n)]
+        kc = at(ke, 1)
+        k = [0.075 * (kc + x) for x in (at(ke, 0), at(ke, 2), roll(kc, DEEP), roll(kc, -DEEP), roll(kc, 1))]
         outer = 0.075 * (kc + jnp.where(top, 0.0, roll(kc, -1)))
         diag = 1.0 - (((k[0] + k[1]) + (k[2] + k[3])) + (k[4] + outer))
         k += [jnp.where(top, 0.0, outer), diag]
-        off = ((i == 0) & (lat == 0)) | ((i == tt + 1) & (lat == n_lat - 1))
-        keep = keep_lane * jnp.where(off, 0.0, 1.0)
-        xf[i] = keep * compact_row(xe[i + 1], xe[i], xe[i + 2], k, xm[i])
-
-        @pl.when((i > 0) & (i < tt + 1))
-        def _():
-            for q in range(7):
-                co[i - 1, q] = k[q]
-
-        return carry
-
-    lax.fori_loop(0, tt + 2, compact_first, 0)
+        row = iota((n, 1, WIDE), 0) + i
+        off = ((row == 0) & (lat == 0)) | ((row == tt + 1) & (lat == n_lat - 1))
+        keep = jnp.where(off, 0.0, keep_lane)
+        xf[pl.ds(i, n)] = keep * compact_rows(at(xe, 1), at(xe, 0), at(xe, 2), k, at(xm, 0))
+        for q in range(7):
+            co[q, pl.ds(i, n)] = k[q]
+        return carry
+
+    lax.fori_loop(0, (tt + 2) // 6, compact_first, 0)
     xm[0:tt] = mixed(xf[1 : tt + 1].reshape(tt * fields, WIDE), tt * fields).reshape(tt, fields, WIDE)
 
-    def compact_second(t, carry):
-        out = compact_row(xf[t + 1], xf[t], xf[t + 2], [co[t, q] for q in range(7)], xm[t])
-        shell[t] = out[:, mid]
-        return carry
-
-    lax.fori_loop(0, tt, compact_second, 0)
+    def compact_second(j, carry):
+        n = 4
+        t = j * n
+        at = lambda ref, d: ref[pl.ds(t + d, n)]
+        k = [co[q, pl.ds(t + 1, n)] for q in range(7)]
+        out = compact_rows(at(xf, 1), at(xf, 0), at(xf, 2), k, at(xm, 0))
+        shell[pl.ds(t, n)] = out[:, :, mid]
+        return carry
+
+    lax.fori_loop(0, tt // 4, compact_second, 0)
     deep_at, cell_at = iota((2 * LANES, LANES), 0), iota((2 * LANES, LANES), 1)
     take = jnp.where(
         (deep_at // DEEP == cell_at // SH) & (deep_at % DEEP == cell_at % SH + DEEP - SH), 1.0, 0.0
@@ -372,31 +379,33 @@
         for f in range(fields + 1):
             side[f, row : row + 1, :] = cr[k, f : f + 1, :]
 
-    def first_row(i, carry):
+    def first_row(i):
         c = ue[:, i + 1]
         low, high = shift_rows(c, pleft[:, pl.ds(7 + i, 1), :], pright[:, pl.ds(7 + i, 1), :])
         up, down = ue[:, i], ue[:, i + 2]
         out = apply_step(
             c[:fields], [x[:fields] for x in (up, down, low, high)],
-            c[fields], [x[fields] for x in (up, down, low, high)], mix,
+            c[fields], [x[fields] for x in (up, down, low, high)], mb,
         )
         off = ((i == 0) & (lat == 0)) | ((i == tt + 1) & (lat == n_lat - 1))
         keep = jnp.where(off, 0.0, 1.0)
-        for g in range(fields):
-            first[g, i] = out[g] * keep
-        return carry
-
-    lax.fori_loop(0, tt + 2, first_row, 0)
+        first[:, i] = out * keep
+
+    def first_pair(j, carry):
+        for h in range(2):
+            first_row(2 * j + h)
+        return carry
+
+    lax.fori_loop(0, (tt + 2) // 2, first_pair, 0)
     for side, outer, inner, into, ok in (
         (pleft, q2.at[0], sp.at[0], fleft, lon > 0),
         (pright, q2.at[1], sp.at[3], fright, lon < n_lon - 1),
     ):
         near = [side[:, 7 : 7 + tt, :], side[:, 9 : 9 + tt, :], outer[...], inner[...]]
         c = side[:, 8 : 8 + tt, :]
-        out = apply_step(c[:fields], [x[:fields] for x in near], c[fields], [x[fields] for x in near], mix)
+        out = apply_step(c[:fields], [x[:fields] for x in near], c[fields], [x[fields] for x in near], mb)
         keep = jnp.where(ok, 1.0, 0.0)
-        for g in range(fields):
-            into[g] = out[g] * keep
+        into[...] = out * keep
 
     other = lax.rem(me + 1, n_dev)
     all_dest = send_to(other, ds.at[0 : n_dev - 1], rd.at[0 : n_dev - 1], dest_send, dest_recv)
@@ -443,7 +452,7 @@
     ]
     launch(edges, face_send, face_recv)
 
-    def second_row(t, carry):
+    def second_row(t):
         c = first[:, t + 1]
         low, high = shift_rows(c, fleft[:, pl.ds(t, 1), :], fright[:, pl.ds(t, 1), :])
         kc = ue[fields:, t + 2]
@@ -452,16 +461,19 @@
         )
         out = apply_step(
             c, [first[:, t], first[:, t + 2], low, high],
-            kc[0], [ue[fields, t + 1], ue[fields, t + 3], klow[0], khigh[0]], mix,
-        )
-        for g in range(fields):
-            st[g, t] = out[g]
+            kc[0], [ue[fields, t + 1], ue[fields, t + 3], klow[0], khigh[0]], mb,
+        )
+        st[:, t] = out
+
+    def second_pair(j, carry):
+        for h in range(2):
+            second_row(2 * j + h)
         return carry
 
     writes = []
     for h in range(2):
         part = slice(h * (tt // 2), (h + 1) * (tt // 2))
-        lax.fori_loop(part.start, part.stop, second_row, 0)
+        lax.fori_loop(part.start // 2, part.stop // 2, second_pair, 0)
         writes.append(pltpu.make_async_copy(st.at[:, part], stepped.at[:, part], out_sem.at[h]))
         writes[h].start()
 
@@ -518,6 +530,7 @@
         scratch_shapes=[
             pltpu.SMEM(mixing.shape, F32),
             v(*mixing.shape),
+            v(fields, fields, 8, LANES),
             v(*helio_prev.shape),
             pltpu.VMEM((1, count), jnp.int32),
             pltpu.VMEM((1, count), jnp.int32),
@@ -528,7 +541,7 @@
             v(tt + 4, 1, WIDE),
             v(tt + 2, fields, WIDE),
             v(tt + 2, fields, WIDE),
-            v(tt, 7, 1, WIDE),
+            v(7, tt + 2, 1, WIDE),
             v(ext, tt + 4, pp, n_r),
             v(4, ext, tt, n_r),
             v(ext, tt + 16, n_r),

time: 29.5 us -> 27 us (0.915)
  Pallas kernels: 27 us -> 24.6 us
    pallas_call x1, Pallas kernels: 27 us -> 24.6 us  [body(): pl.pallas_call(functools.partial(kernel, n_lat, n_lon), out_shape=(jax.Sh...]
where the time goes in v5:
time: 27 us; the launch traced here: 26.9 us
  Pallas kernels  24.6 us (91%)
  local copies, waits for them, and re-layouts  1.63 us (6%)
  between operations  0.64 us (2%)
    pallas_call x1, Pallas kernels, body(): pl.pallas_call(functools.partial(kernel, n_lat, n_lon), out_shape=(jax.Sh...  24.6 us
    unnamed x2, local copies, waits for them, and re-layouts  1.63 us

profile of v5, /device:TPU:0, one launch (start us, length us, event | category | flops | bytes accessed | tf_op | source)
XLA Modules:
  0.0 26.9 jit_solution(17776681763731923271)
XLA Ops:
  0.6 24.6 %corona_helio.1 = (f32[8,16,16,128]{3,2,1,0:T(8,128)S(1)}, f32[8,32,128]{2,1,0:T(8,128)S(1)}) custom-call(f32[8,16,16,128]{3,2,1,0:T(8,128)} %corona.1, f32[16,16,128]{2,1,0:T(8,128)} %kappa.1, f32[8,8]{1,0:T(8,128)} %mix_in.1, f32[8,32,128]{2,1,0:T(8,128)} %helio_in.1, s32[1,2048]{1,0:T(1,128)} %bitcast.3, s32[1,2048]{1,0:T(1,128)} %bitcast.4, ...), custom_call_target="tpu_custom_call" | custom-call | tf_op jit(solution)/shard_map/corona_helio/pallas_call | solution.py:522
  25.2 1.0 %copy.12 = f32[8,16,16,128]{3,2,1,0:T(8,128)} copy(f32[8,16,16,128]{3,2,1,0:T(8,128)S(1)} %get-tuple-element.4) | data formatting | bytes 2097152
  26.2 0.7 %copy.13 = f32[8,32,128]{2,1,0:T(8,128)} copy(f32[8,32,128]{2,1,0:T(8,128)S(1)} %get-tuple-element.5) | data formatting | bytes 262144

commit v6 on v5

--- a/solution.py
+++ b/solution.py
@@ -13,7 +13,7 @@
 MESH = pl.DeviceIdType.MESH
 LANES = 128
 GROUP = 8
-LAND = 4
+LAND = 8
 NPAR = 5
 DEEP = 16
 WIDE = 4 * LANES
@@ -291,9 +291,9 @@
     def roll(x, by):
         return pltpu.roll(x, by % WIDE, 2)
 
-    def compact_rows(c, up, down, k, more):
+    def compact_rows(c, up, down, k):
         return (
-            more + k[6] * c + (k[0] * up + k[1] * down) + (k[2] * roll(c, DEEP) + k[3] * roll(c, -DEEP))
+            k[6] * c + (k[0] * up + k[1] * down) + (k[2] * roll(c, DEEP) + k[3] * roll(c, -DEEP))
             + (k[4] * roll(c, 1) + k[5] * roll(c, -1))
         )
 
@@ -309,21 +309,23 @@
         row = iota((n, 1, WIDE), 0) + i
         off = ((row == 0) & (lat == 0)) | ((row == tt + 1) & (lat == n_lat - 1))
         keep = jnp.where(off, 0.0, keep_lane)
-        xf[pl.ds(i, n)] = keep * compact_rows(at(xe, 1), at(xe, 0), at(xe, 2), k, at(xm, 0))
+        xf[pl.ds(i, n)] = keep * (compact_rows(at(xe, 1), at(xe, 0), at(xe, 2), k) + at(xm, 0))
         for q in range(7):
             co[q, pl.ds(i, n)] = k[q]
         return carry
 
     lax.fori_loop(0, (tt + 2) // 6, compact_first, 0)
-    xm[0:tt] = mixed(xf[1 : tt + 1].reshape(tt * fields, WIDE), tt * fields).reshape(tt, fields, WIDE)
+    half_wide = 2 * LANES
+    again = mixed(xf[1 : tt + 1, :, mid].reshape(tt * fields, half_wide), tt * fields)
+    xm[0:tt, :, 0:half_wide] = again.reshape(tt, fields, half_wide)
 
     def compact_second(j, carry):
         n = 4
         t = j * n
         at = lambda ref, d: ref[pl.ds(t + d, n)]
         k = [co[q, pl.ds(t + 1, n)] for q in range(7)]
-        out = compact_rows(at(xf, 1), at(xf, 0), at(xf, 2), k, at(xm, 0))
-        shell[pl.ds(t, n)] = out[:, :, mid]
+        out = compact_rows(at(xf, 1), at(xf, 0), at(xf, 2), k)
+        shell[pl.ds(t, n)] = out[:, :, mid] + xm[pl.ds(t, n), :, 0:half_wide]
         return carry
 
     lax.fori_loop(0, tt // 4, compact_second, 0)
@@ -387,16 +389,20 @@
             c[:fields], [x[:fields] for x in (up, down, low, high)],
             c[fields], [x[fields] for x in (up, down, low, high)], mb,
         )
-        off = ((i == 0) & (lat == 0)) | ((i == tt + 1) & (lat == n_lat - 1))
-        keep = jnp.where(off, 0.0, 1.0)
-        first[:, i] = out * keep
-
-    def first_pair(j, carry):
-        for h in range(2):
-            first_row(2 * j + h)
-        return carry
-
-    lax.fori_loop(0, (tt + 2) // 2, first_pair, 0)
+        first[:, i] = out
+
+    def first_rows(j, carry):
+        for h in range(3):
+            first_row(3 * j + h)
+        return carry
+
+    lax.fori_loop(0, (tt + 2) // 3, first_rows, 0)
+    for i, edge in ((0, 0), (tt + 1, n_lat - 1)):
+
+        @pl.when(lat == edge)
+        def _(i=i):
+            first[:, i] = jnp.zeros((fields, pp, first.shape[3]), F32)
+
     for side, outer, inner, into, ok in (
         (pleft, q2.at[0], sp.at[0], fleft, lon > 0),
         (pright, q2.at[1], sp.at[3], fright, lon < n_lon - 1),
@@ -465,15 +471,15 @@
         )
         st[:, t] = out
 
-    def second_pair(j, carry):
-        for h in range(2):
-            second_row(2 * j + h)
+    def second_rows(j, carry):
+        for h in range(4):
+            second_row(4 * j + h)
         return carry
 
     writes = []
     for h in range(2):
         part = slice(h * (tt // 2), (h + 1) * (tt // 2))
-        lax.fori_loop(part.start // 2, part.stop // 2, second_pair, 0)
+        lax.fori_loop(part.start // 4, part.stop // 4, second_rows, 0)
         writes.append(pltpu.make_async_copy(st.at[:, part], stepped.at[:, part], out_sem.at[h]))
         writes[h].start()
 

time: 27 us -> 26.3 us (0.974)
  Pallas kernels: 24.6 us -> 23.9 us
    pallas_call x1, Pallas kernels: 24.6 us -> 23.9 us  [body(): pl.pallas_call(functools.partial(kernel, n_lat, n_lon), out_shape=(jax.Sh...]
where the time goes in v6:
time: 26.3 us; the launch traced here: 26.1 us
  Pallas kernels  23.9 us (91%)
  local copies, waits for them, and re-layouts  1.63 us (6%)
  between operations  0.64 us (2%)
    pallas_call x1, Pallas kernels, body(): pl.pallas_call(functools.partial(kernel, n_lat, n_lon), out_shape=(jax.Sh...  23.9 us
    unnamed x2, local copies, waits for them, and re-layouts  1.63 us

profile of v6, /device:TPU:0, one launch (start us, length us, event | category | flops | bytes accessed | tf_op | source)
XLA Modules:
  0.0 26.1 jit_solution(4611259464449409453)
XLA Ops:
  0.6 23.9 %corona_helio.1 = (f32[8,16,16,128]{3,2,1,0:T(8,128)S(1)}, f32[8,32,128]{2,1,0:T(8,128)S(1)}) custom-call(f32[8,16,16,128]{3,2,1,0:T(8,128)} %corona.1, f32[16,16,128]{2,1,0:T(8,128)} %kappa.1, f32[8,8]{1,0:T(8,128)} %mix_in.1, f32[8,32,128]{2,1,0:T(8,128)} %helio_in.1, s32[1,2048]{1,0:T(1,128)} %bitcast.3, s32[1,2048]{1,0:T(1,128)} %bitcast.4, ...), custom_call_target="tpu_custom_call" | custom-call | tf_op jit(solution)/shard_map/corona_helio/pallas_call | solution.py:528
  24.5 1.0 %copy.12 = f32[8,16,16,128]{3,2,1,0:T(8,128)} copy(f32[8,16,16,128]{3,2,1,0:T(8,128)S(1)} %get-tuple-element.4) | data formatting | bytes 2097152
  25.5 0.7 %copy.13 = f32[8,32,128]{2,1,0:T(8,128)} copy(f32[8,32,128]{2,1,0:T(8,128)S(1)} %get-tuple-element.5) | data formatting | bytes 262144

commit v7 on v6

--- a/solution.py
+++ b/solution.py
@@ -337,7 +337,9 @@
         jnp.dot(x, take, preferred_element_type=F32).astype(BF16)
         for x in split(shell[...].reshape(tt * fields, 2 * LANES))
     ]
-    left = jnp.concatenate([s_hi, s_hi, s_lo], axis=1)
+    left = jnp.concatenate(
+        [jnp.concatenate([s_hi, s_hi], axis=1), jnp.concatenate([s_lo, jnp.zeros_like(s_lo)], axis=1)], axis=0
+    )
     groups = n_dev // GROUP
     wide = GROUP * LANES
 
@@ -358,7 +360,8 @@
         wa, wb, wc = weights(tt, t0, fx), weights(pp, p0, fy), weights(SH, r0, fz)
         table = (wb[:, None, :] * wc[None]).reshape(pp * SH, wide)
         hi, lo = split(table)
-        got = jnp.dot(left, jnp.concatenate([hi, lo, hi], axis=0), preferred_element_type=F32)
+        got = jnp.dot(left, jnp.concatenate([hi, lo], axis=0), preferred_element_type=F32)
+        got = got[: tt * fields] + got[tt * fields :]
         val = jnp.sum(got.reshape(tt, fields, wide) * wa[:, None, :], axis=0)
         for k in range(GROUP):
             vs[g * GROUP + k] = val[:, k * LANES : (k + 1) * LANES]
@@ -420,14 +423,17 @@
     all_vals.wait_recv()
 
     face_p, face_t = helio.shape[1], helio.shape[2]
+    rows_p = face_p // 2
     acc[...] = jnp.zeros(acc.shape, F32)
 
     def land(i, carry):
         cell = jnp.concatenate([rd[i * LAND + k] for k in range(LAND)], axis=1).astype(jnp.int32) - 1
         val = jnp.concatenate([rv[i * LAND + k] for k in range(LAND)], axis=1)
         hi = val.astype(BF16).astype(F32)
-        on_p = iota((face_p, LAND * LANES), 0) == (cell >> 7)
-        on_t = jnp.where(iota((face_t, LAND * LANES), 0) == (cell & 127), 1.0, 0.0).astype(BF16)
+        low_p = jnp.where(cell < 0, -1, (cell >> 7) & (rows_p - 1))
+        column = (cell & 127) + (cell >> 11) * face_t
+        on_p = iota((rows_p, LAND * LANES), 0) == low_p
+        on_t = jnp.where(iota((2 * face_t, LAND * LANES), 0) == column, 1.0, 0.0).astype(BF16)
         spread = jnp.concatenate(
             [jnp.where(on_p, x[f : f + 1], 0.0).astype(BF16) for x in (hi, val - hi) for f in range(fields)],
             axis=0,
@@ -436,9 +442,10 @@
         return carry
 
     lax.fori_loop(0, n_dev // LAND, land, 0)
-    half = fields * face_p
-    flat = helio[...].reshape(half, face_t) + (acc[0:half] + acc[half:])
-    coupled = flat.reshape(fields, face_p, face_t)
+    half = fields * rows_p
+    added = (acc[0:half] + acc[half:]).reshape(fields, rows_p, 2 * face_t)
+    coupled = helio[...] + jnp.concatenate([added[:, :, :face_t], added[:, :, face_t:]], axis=1)
+    flat = coupled.reshape(fields * face_p, face_t)
 
     for f in range(fields):
         hs[0, f : f + 1, :] = coupled[f, 0:1, :]
@@ -569,7 +576,7 @@
             v(2, fields, face_t),
             v(8, fields * face_p),
             v(2, 8, fields * face_p),
-            v(2 * fields * face_p, face_t),
+            v(fields * face_p, 2 * face_t),
             sem((9,)), sem((10,)), sem((10,)), sem((16,)), sem((16,)), sem((2,)), sem,
             sem, sem, sem, sem, sem((4,)), sem((4,)),
         ],

time: 26.3 us -> 25.9 us (0.985)
  Pallas kernels: 23.9 us -> 23.5 us
    pallas_call x1, Pallas kernels: 23.9 us -> 23.5 us  [body(): pl.pallas_call(functools.partial(kernel, n_lat, n_lon), out_shape=(jax.Sh...]
where the time goes in v7:
time: 25.9 us; the launch traced here: 25.8 us
  Pallas kernels  23.5 us (91%)
  local copies, waits for them, and re-layouts  1.63 us (6%)
  between operations  0.64 us (2%)
    pallas_call x1, Pallas kernels, body(): pl.pallas_call(functools.partial(kernel, n_lat, n_lon), out_shape=(jax.Sh...  23.5 us
    unnamed x2, local copies, waits for them, and re-layouts  1.63 us

profile of v7, /device:TPU:0, one launch (start us, length us, event | category | flops | bytes accessed | tf_op | source)
XLA Modules:
  0.0 25.8 jit_solution(9169269007911673378)
XLA Ops:
  0.6 23.5 %corona_helio.1 = (f32[8,16,16,128]{3,2,1,0:T(8,128)S(1)}, f32[8,32,128]{2,1,0:T(8,128)S(1)}) custom-call(f32[8,16,16,128]{3,2,1,0:T(8,128)} %corona.1, f32[16,16,128]{2,1,0:T(8,128)} %kappa.1, f32[8,8]{1,0:T(8,128)} %mix_in.1, f32[8,32,128]{2,1,0:T(8,128)} %helio_in.1, s32[1,2048]{1,0:T(1,128)} %bitcast.3, s32[1,2048]{1,0:T(1,128)} %bitcast.4, ...), custom_call_target="tpu_custom_call" | custom-call | tf_op jit(solution)/shard_map/corona_helio/pallas_call | solution.py:535
  24.1 1.0 %copy.12 = f32[8,16,16,128]{3,2,1,0:T(8,128)} copy(f32[8,16,16,128]{3,2,1,0:T(8,128)S(1)} %get-tuple-element.4) | data formatting | bytes 2097152
  25.1 0.7 %copy.13 = f32[8,32,128]{2,1,0:T(8,128)} copy(f32[8,32,128]{2,1,0:T(8,128)S(1)} %get-tuple-element.5) | data formatting | bytes 262144
